TPU v7x, 32 devices: a whole 2x2x4 slice. The times are simulated.
32 devices in a mesh: dp: 4 (over z), freq: 8 (over y, x, core).
Axes of the slice: x: 2, y: 2, z: 4, core: 2. Of those that a mesh axis runs over, the one named last changes fastest.
Arguments:
- tokens: bfloat16 [8, 2048, 768], P('dp', 'freq'), may hold values from -6 to 6
- offsets: int32 [8], P('dp'), may hold values from 0 to 1023, as said below
- kernel_lengths: int32 [768], replicated, may hold values from 512 to 2048, as said below
- norm1_gain: float32 [768], replicated, may hold values from 0.5 to 1.5
- norm1_bias: float32 [768], replicated, may hold values from -3 to 3
- input_projection_weight: bfloat16 [768, 2304], replicated, may hold values from -0.21875 to 0.21875
- in_bias: float32 [2304], replicated, may hold values from -2 to 2
- kernel_taps: float32 [768, 2048], P(None, 'freq'), may hold values from -0.25 to 0.25
- skip_gain: float32 [768], P('freq'), may hold values from -3 to 3
- out_weight: bfloat16 [768, 768], replicated, may hold values from -0.21875 to 0.21875
- out_bias: float32 [768], replicated, may hold values from -2 to 2
- norm2_gain: float32 [768], replicated, may hold values from 0.5 to 1.5
- norm2_bias: float32 [768], replicated, may hold values from -3 to 3
- up_projection_weight: bfloat16 [768, 3072], replicated, may hold values from -0.21875 to 0.21875
- fc1_bias: float32 [3072], replicated, may hold values from -2 to 2
- down_projection_weight: bfloat16 [3072, 768], replicated, may hold values from -0.109375 to 0.109375
- fc2_bias: float32 [768], replicated, may hold values from -2 to 2
- cotangent: bfloat16 [8, 2048, 768], P('dp', 'freq'), may hold values from -6 to 6
Outputs:
- block_out: bfloat16 [8, 2048, 768], P('dp', 'freq')
- input_grad: bfloat16 [8, 2048, 768], P('dp', 'freq')
- norm1_gain_grad: float32 [768], P('freq')
- norm1_bias_grad: float32 [768], P('freq')
- in_weight_grad: float32 [768, 2304], P('dp', 'freq')
- in_bias_grad: float32 [2304], P('freq')
- kernel_taps_grad: float32 [768, 2048], P(None, 'freq')
- skip_grad: float32 [768], P('freq')
- out_weight_grad: float32 [768, 768], P('dp', 'freq')
- out_bias_grad: float32 [768], P('freq')
- norm2_gain_grad: float32 [768], P('freq')
- norm2_bias_grad: float32 [768], P('freq')
- fc1_weight_grad: float32 [768, 3072], P('dp', 'freq')
- fc1_bias_grad: float32 [3072], P('freq')
- fc2_weight_grad: float32 [3072, 768], P('dp', 'freq')
- fc2_bias_grad: float32 [768], P('freq')
Inputs may be any that keep to these rules, and one draw needn't show every extreme that they name: `offsets`: in every run of 2 consecutive sequences (those of one index of dp) at least one has offset 0; some sequence has offset 2048 / 2 - 1. `kernel_lengths`: at least one channel's kernel has all 2048 taps.
All inputs are finite; a program needn't handle non-finite values.
Results may differ from a plain program's by a relative error of at most 0.018.
Values may be sent and summed in bfloat16 or wider, within the bound.
No kernel may reach another device: no remote copies, remote signals or barrier semaphores. Data moves between devices by JAX's collectives and lax.ppermute only.
A program may use at most 192 MiB of HBM per device.

v0:
```python
import jax
import jax.numpy as jnp
from jax import lax
from jax.sharding import PartitionSpec as P

NORM_EPS = 1e-05
SHRINK = 0.003
PRECISE = lax.Precision.HIGHEST


def extended(block, sides, width):
    for axis, dim in sides:
        count = lax.axis_size(axis)
        forward = [(i, i + 1) for i in range(count - 1)]
        backward = [(target, source) for source, target in forward]
        low = lax.ppermute(
            lax.slice_in_dim(block, block.shape[dim] - width, None, axis=dim), axis, forward
        )
        high = lax.ppermute(lax.slice_in_dim(block, 0, width, axis=dim), axis, backward)
        block = jnp.concatenate([low, block, high], axis=dim)
    return block


def layer_norm(values, norm_gain, norm_shift):
    centred = values - jnp.mean(values, axis=-1, keepdims=True)
    spread = jnp.mean(centred * centred, axis=-1, keepdims=True)
    return centred * lax.rsqrt(spread + NORM_EPS) * norm_gain + norm_shift


def gelu_tanh(values):
    return jax.nn.gelu(values, approximate=True)


def angle_table(left_index, right_index, period):
    product = left_index[:, None] * right_index[None, :] % period
    angles = product.astype(jnp.float32) * (2.0 * jnp.pi / period)
    return (jnp.cos(angles), jnp.sin(angles))


def dft_tables(outer_size, inner_width):
    upper_rows = jnp.arange(outer_size // 2, dtype=jnp.int32)
    across = jnp.arange(outer_size, dtype=jnp.int32)
    within = jnp.arange(inner_width, dtype=jnp.int32)
    outer_cos, outer_sin = angle_table(upper_rows, across, outer_size)
    inner_cos, inner_sin = angle_table(within, within, inner_width)
    twist_cos, twist_sin = angle_table(across, within, outer_size * inner_width)
    return (outer_cos, outer_sin, inner_cos, inner_sin, twist_cos, twist_sin)


def forward_dft(signal, tables):
    outer_cos, outer_sin, inner_cos, inner_sin, twist_cos, twist_sin = tables
    half_rows = outer_cos.shape[0]
    inner_width = inner_cos.shape[0]
    folded = signal.reshape(signal.shape[:-1] + (half_rows, inner_width))
    real_first = jnp.einsum("...nm,nk->...km", folded, outer_cos, precision=PRECISE)
    imag_first = -jnp.einsum("...nm,nk->...km", folded, outer_sin, precision=PRECISE)
    real_twist = real_first * twist_cos + imag_first * twist_sin
    imag_twist = imag_first * twist_cos - real_first * twist_sin
    real_out = jnp.einsum("...km,mj->...kj", real_twist, inner_cos, precision=PRECISE) + jnp.einsum(
        "...km,mj->...kj", imag_twist, inner_sin, precision=PRECISE
    )
    imag_out = jnp.einsum("...km,mj->...kj", imag_twist, inner_cos, precision=PRECISE) - jnp.einsum(
        "...km,mj->...kj", real_twist, inner_sin, precision=PRECISE
    )
    return (real_out, imag_out)


def inverse_dft(real_in, imag_in, tables):
    outer_cos, outer_sin, inner_cos, inner_sin, twist_cos, twist_sin = tables
    half_rows = outer_cos.shape[0]
    outer_size = outer_cos.shape[1]
    inner_width = inner_cos.shape[0]
    real_first = jnp.einsum("...kj,jm->...km", real_in, inner_cos, precision=PRECISE) - jnp.einsum(
        "...kj,jm->...km", imag_in, inner_sin, precision=PRECISE
    )
    imag_first = jnp.einsum("...kj,jm->...km", imag_in, inner_cos, precision=PRECISE) + jnp.einsum(
        "...kj,jm->...km", real_in, inner_sin, precision=PRECISE
    )
    real_twist = real_first * twist_cos - imag_first * twist_sin
    imag_twist = imag_first * twist_cos + real_first * twist_sin
    signal = jnp.einsum("...km,nk->...nm", real_twist, outer_cos, precision=PRECISE) - jnp.einsum(
        "...km,nk->...nm", imag_twist, outer_sin, precision=PRECISE
    )
    signal = signal.reshape(signal.shape[:-2] + (half_rows * inner_width,))
    return signal / (outer_size * inner_width)


def body(
    tokens,
    offsets,
    kernel_lengths,
    norm1_gain,
    norm1_bias,
    input_projection_weight,
    in_bias,
    kernel_taps,
    skip_gain,
    out_weight,
    out_bias,
    norm2_gain,
    norm2_bias,
    up_projection_weight,
    fc1_bias,
    down_projection_weight,
    fc2_bias,
    cotangent,
):
    freq_parts = lax.axis_size("freq")
    tok_rows = tokens.shape[1]
    model_width = tokens.shape[2]
    full_len = tok_rows * freq_parts
    tap_rows = kernel_taps.shape[1]
    taps_all = tap_rows * freq_parts
    tables = dft_tables(freq_parts, 2 * tok_rows)
    tap_index = lax.axis_index("freq") * tap_rows + jnp.arange(tap_rows, dtype=jnp.int32)
    tap_keep = (tap_index[None, :] < kernel_lengths[:, None]).astype(jnp.float32)
    shrunk = kernel_taps - SHRINK * jnp.tanh(kernel_taps / SHRINK)
    rimmed = extended(shrunk.astype(jnp.bfloat16), (("freq", 1),), 1).astype(shrunk.dtype)
    pooled = (rimmed[:, :-2] + rimmed[:, 1:-1] + rimmed[:, 2:]) / 3.0 * tap_keep
    kernel_chan = lax.all_to_all(
        pooled.astype(jnp.bfloat16), "freq", split_axis=0, concat_axis=1, tiled=True
    ).astype(pooled.dtype)
    kernel_pad = jnp.pad(kernel_chan, ((0, 0), (0, full_len - taps_all)))
    kernel_real, kernel_imag = forward_dft(kernel_pad, tables)
    inputs = tokens.astype(jnp.float32)
    first_normalized_input = layer_norm(inputs, norm1_gain, norm1_bias).astype(jnp.bfloat16)
    projected = (
        jnp.einsum(
            "ugy,yj->ujg",
            first_normalized_input,
            input_projection_weight,
            preferred_element_type=jnp.float32,
        )
        + in_bias[None, :, None]
    )
    value_part = projected[:, :model_width]
    first_gate = projected[:, model_width : 2 * model_width]
    second_gate = projected[:, 2 * model_width :]
    positions = lax.axis_index("freq") * tok_rows + jnp.arange(tok_rows, dtype=jnp.int32)
    live_mask = (positions[None, None, :] >= offsets[:, None, None]).astype(jnp.float32)
    mixed_in = (live_mask * first_gate * value_part).astype(jnp.bfloat16)
    mixed_chan = lax.all_to_all(mixed_in, "freq", split_axis=1, concat_axis=2, tiled=True).astype(
        jnp.float32
    )
    mixed_real, mixed_imag = forward_dft(mixed_chan, tables)
    conv_chan = inverse_dft(
        mixed_real * kernel_real - mixed_imag * kernel_imag,
        mixed_real * kernel_imag + mixed_imag * kernel_real,
        tables,
    )
    skip_column = skip_gain[:, None]
    conv_chan = (conv_chan + skip_column * mixed_chan).astype(jnp.bfloat16)
    conv_out = lax.all_to_all(conv_chan, "freq", split_axis=2, concat_axis=1, tiled=True).astype(
        jnp.float32
    )
    gated = (second_gate * conv_out).astype(jnp.bfloat16)
    branch = (
        jnp.einsum("bdq,de->bqe", gated, out_weight, preferred_element_type=jnp.float32) + out_bias
    )
    residual = inputs + branch
    second_normalized_input = layer_norm(residual, norm2_gain, norm2_bias).astype(jnp.bfloat16)
    hidden = (
        jnp.einsum(
            "mrj,jy->mry",
            second_normalized_input,
            up_projection_weight,
            preferred_element_type=jnp.float32,
        )
        + fc1_bias
    )
    gelu_activation = gelu_tanh(hidden).astype(jnp.bfloat16)
    block_out = (
        residual
        + jnp.einsum(
            "cpi,ih->cph",
            gelu_activation,
            down_projection_weight,
            preferred_element_type=jnp.float32,
        )
        + fc2_bias
    ).astype(jnp.bfloat16)
    upstream = cotangent.astype(jnp.float32)
    down_projection_gradient = jnp.einsum(
        "orn,orv->nv", gelu_activation, cotangent, preferred_element_type=jnp.float32
    )
    grad_bias_two = jnp.sum(upstream, axis=(0, 1))
    active_grad = jnp.einsum(
        "rig,pg->rip", cotangent, down_projection_weight, preferred_element_type=jnp.float32
    )
    gelu_pull = jax.vjp(gelu_tanh, hidden)[1]
    hidden_units_gradient = gelu_pull(active_grad)[0].astype(jnp.bfloat16)
    grad_fc_one = jnp.einsum(
        "zsk,zso->ko",
        second_normalized_input,
        hidden_units_gradient,
        preferred_element_type=jnp.float32,
    )
    grad_bias_one = jnp.sum(hidden_units_gradient.astype(jnp.float32), axis=(0, 1))
    normed_two_grad = jnp.einsum(
        "jtl,hl->jth",
        hidden_units_gradient,
        up_projection_weight,
        preferred_element_type=jnp.float32,
    )
    norm_pull_two = jax.vjp(layer_norm, residual, norm2_gain, norm2_bias)[1]
    residual_norm, grad_gain_two, grad_shift_two = norm_pull_two(normed_two_grad)
    residual_grad = upstream + residual_norm
    branch_grad = residual_grad.astype(jnp.bfloat16)
    grad_out_w = jnp.einsum("bdq,bqe->de", gated, branch_grad, preferred_element_type=jnp.float32)
    grad_out_bias = jnp.sum(branch_grad.astype(jnp.float32), axis=(0, 1))
    gated_grad = jnp.einsum(
        "bqe,de->bdq", branch_grad, out_weight, preferred_element_type=jnp.float32
    )
    second_grad = gated_grad * conv_out
    conv_grad = (gated_grad * second_gate).astype(jnp.bfloat16)
    conv_grad_chan = lax.all_to_all(
        conv_grad, "freq", split_axis=1, concat_axis=2, tiled=True
    ).astype(jnp.float32)
    grad_real, grad_imag = forward_dft(conv_grad_chan, tables)
    mixed_grad_chan = inverse_dft(
        grad_real * kernel_real + grad_imag * kernel_imag,
        grad_imag * kernel_real - grad_real * kernel_imag,
        tables,
    )
    mixed_grad_chan = (mixed_grad_chan + skip_column * conv_grad_chan).astype(jnp.bfloat16)
    skip_grad = jnp.sum(conv_grad_chan * mixed_chan, axis=(0, 2))
    taps_real = jnp.sum(grad_real * mixed_real + grad_imag * mixed_imag, axis=0)
    taps_imag = jnp.sum(grad_imag * mixed_real - grad_real * mixed_imag, axis=0)
    pooled_grad_chan = inverse_dft(taps_real, taps_imag, tables)[:, :taps_all]
    pooled_grad = (
        lax.all_to_all(
            pooled_grad_chan.astype(jnp.bfloat16), "freq", split_axis=1, concat_axis=0, tiled=True
        ).astype(pooled_grad_chan.dtype)
        * tap_keep
    )
    rimmed_grad = extended(pooled_grad.astype(jnp.bfloat16), (("freq", 1),), 1).astype(
        pooled_grad.dtype
    )
    taps_grad = (
        (rimmed_grad[:, :-2] + rimmed_grad[:, 1:-1] + rimmed_grad[:, 2:])
        / 3.0
        * jnp.square(jnp.tanh(kernel_taps / SHRINK))
    )
    mixed_grad = lax.all_to_all(
        mixed_grad_chan, "freq", split_axis=2, concat_axis=1, tiled=True
    ).astype(jnp.float32)
    value_grad = live_mask * first_gate * mixed_grad
    first_grad = live_mask * value_part * mixed_grad
    projection_output_gradient = jnp.concatenate(
        [value_grad, first_grad, second_grad], axis=1
    ).astype(jnp.bfloat16)
    grad_in_w = jnp.einsum(
        "xjm,xcj->mc",
        first_normalized_input,
        projection_output_gradient,
        preferred_element_type=jnp.float32,
    )
    grad_in_bias = jnp.sum(projection_output_gradient.astype(jnp.float32), axis=(0, 2))
    normed_grad = jnp.einsum(
        "mtj,xt->mjx",
        projection_output_gradient,
        input_projection_weight,
        preferred_element_type=jnp.float32,
    )
    norm_pull_one = jax.vjp(layer_norm, inputs, norm1_gain, norm1_bias)[1]
    input_norm, grad_gain_one, grad_shift_one = norm_pull_one(normed_grad)
    input_grad = (residual_grad + input_norm).astype(jnp.bfloat16)
    gain_one_row = grad_gain_one.reshape(1, -1)
    shift_one_row = grad_shift_one.reshape(1, -1)
    in_bias_row = grad_in_bias.reshape(1, -1)
    out_bias_row = grad_out_bias.reshape(1, -1)
    gain_two_row = grad_gain_two.reshape(1, -1)
    shift_two_row = grad_shift_two.reshape(1, -1)
    bias_one_row = grad_bias_one.reshape(1, -1)
    bias_two_row = grad_bias_two.reshape(1, -1)
    summed = (
        lax.psum_scatter(grad_in_w, "freq", scatter_dimension=1, tiled=True),
        lax.psum_scatter(grad_out_w, "freq", scatter_dimension=1, tiled=True),
        lax.psum_scatter(grad_fc_one, "freq", scatter_dimension=1, tiled=True),
        lax.psum_scatter(down_projection_gradient, "freq", scatter_dimension=1, tiled=True),
        lax.psum_scatter(gain_one_row, "freq", scatter_dimension=1, tiled=True),
        lax.psum_scatter(shift_one_row, "freq", scatter_dimension=1, tiled=True),
        lax.psum_scatter(in_bias_row, "freq", scatter_dimension=1, tiled=True),
        lax.psum_scatter(out_bias_row, "freq", scatter_dimension=1, tiled=True),
        lax.psum_scatter(gain_two_row, "freq", scatter_dimension=1, tiled=True),
        lax.psum_scatter(shift_two_row, "freq", scatter_dimension=1, tiled=True),
        lax.psum_scatter(bias_one_row, "freq", scatter_dimension=1, tiled=True),
        lax.psum_scatter(bias_two_row, "freq", scatter_dimension=1, tiled=True),
    )
    matrices = (
        lax.psum_scatter(
            summed[0].astype(jnp.bfloat16), "dp", scatter_dimension=0, tiled=True
        ).astype(jnp.float32),
        lax.psum_scatter(
            summed[1].astype(jnp.bfloat16), "dp", scatter_dimension=0, tiled=True
        ).astype(jnp.float32),
        lax.psum_scatter(
            summed[2].astype(jnp.bfloat16), "dp", scatter_dimension=0, tiled=True
        ).astype(jnp.float32),
        lax.psum_scatter(
            summed[3].astype(jnp.bfloat16), "dp", scatter_dimension=0, tiled=True
        ).astype(jnp.float32),
    )
    smaller = (
        lax.psum(summed[4].astype(jnp.bfloat16), "dp").astype(jnp.float32),
        lax.psum(summed[5].astype(jnp.bfloat16), "dp").astype(jnp.float32),
        lax.psum(summed[6].astype(jnp.bfloat16), "dp").astype(jnp.float32),
        lax.psum(summed[7].astype(jnp.bfloat16), "dp").astype(jnp.float32),
        lax.psum(summed[8].astype(jnp.bfloat16), "dp").astype(jnp.float32),
        lax.psum(summed[9].astype(jnp.bfloat16), "dp").astype(jnp.float32),
        lax.psum(summed[10].astype(jnp.bfloat16), "dp").astype(jnp.float32),
        lax.psum(summed[11].astype(jnp.bfloat16), "dp").astype(jnp.float32),
        lax.psum(taps_grad.astype(jnp.bfloat16), "dp").astype(jnp.float32),
        lax.psum(skip_grad.astype(jnp.bfloat16), "dp").astype(jnp.float32),
    )
    vectors = smaller[:8]
    taps_final = smaller[8]
    skip_final = smaller[9]
    return (
        block_out,
        input_grad,
        vectors[0].reshape(-1),
        vectors[1].reshape(-1),
        matrices[0],
        vectors[2].reshape(-1),
        taps_final,
        skip_final,
        matrices[1],
        vectors[3].reshape(-1),
        vectors[4].reshape(-1),
        vectors[5].reshape(-1),
        matrices[2],
        vectors[6].reshape(-1),
        matrices[3],
        vectors[7].reshape(-1),
    )


def solution(mesh):
    in_specs = (
        P("dp", "freq", None),
        P("dp"),
        P(),
        P(),
        P(),
        P(),
        P(),
        P(None, "freq"),
        P("freq"),
        P(),
        P(),
        P(),
        P(),
        P(),
        P(),
        P(),
        P(),
        P("dp", "freq", None),
    )
    out_specs = (
        P("dp", "freq", None),
        P("dp", "freq", None),
        P("freq"),
        P("freq"),
        P("dp", "freq"),
        P("freq"),
        P(None, "freq"),
        P("freq"),
        P("dp", "freq"),
        P("freq"),
        P("freq"),
        P("freq"),
        P("dp", "freq"),
        P("freq"),
        P("dp", "freq"),
        P("freq"),
    )
    return jax.shard_map(body, mesh=mesh, in_specs=in_specs, out_specs=out_specs, check_vma=False)
```

profile of v0, /device:TPU:0, one launch (start us, length us, event | category | flops | bytes accessed | tf_op | source)
XLA Modules:
  0.0 1042.8 jit_solution(16166848136212575136)
XLA Ops:
  26.6 6.4 all-to-all-start.1
  54.2 6.7 fusion.81
  60.9 7.9 fusion.103
  68.8 6.6 fusion.79
  75.5 7.8 fusion.106
  94.5 9.6 fusion.29
  104.1 9.4 fusion.27
  113.6 9.7 fusion.57
  123.3 9.9 fusion.60
  133.2 9.6 fusion.147
  142.9 9.4 fusion.149
  153.7 9.7 convolution_add_fusion.2
  163.4 9.9 convolution_subtract_fusion.1
  190.1 19.8 %all_to_all.74 = bf16[2,96,2048]{1,0,2:T(2,128)(2,1)} all-to-all(bf16[2,96,2048]{1,0,2:T(2,128)(2,1)} %copy.98), channel_id=1, replica_groups=mesh['dp'=4,'freq'=8] {'freq'}, dimensions={2} | all-to-all | bytes 1572864 | tf_op jit(solution)/shard_map/all_to_all | solution.py:153
  223.4 5.6 fusion.14
  229.1 7.2 convert_reduce_fusion
  256.4 8.9 all-to-all-done.3
  276.4 11.2 %fusion.21 = f32[2,96,8,512]{3,2,1,0:T(8,128)} fusion(f32[8,2,96,512]{3,0,2,1:T(8,128)S(1)} %fusion.229, f32[8,2,96,512]{3,0,2,1:T(8,128)S(1)} %fusion.218, f32[8,512]{1,0:T(8,128)S(1)} %get-tuple-element.119, f32[8,512]{1,0:T(8,128)S(1)} %copy-done.21), kind=kOutput, calls=%fused_computation.30 | convolution fusion | flops 4838653952 | bytes 9469952 | tf_op jit(solution)/shard_map/...km,mj->...kj/dot_general | solution.py:59
  287.6 9.2 fusion.19
  296.8 9.4 fusion.66
  306.3 16.6 %subtract_reduce_fusion = (f32[96,8,512]{2,1,0:T(8,128)}, f32[96,8,512]{2,1,0:T(8,128)}, f32[2,96,8,512]{3,2,1,0:T(8,128)S(1)}) fusion(f32[2,96,8,512]{3,2,1,0:T(8,128)S(1)} %copy-done.8, f32[2,96,8,512]{3,2,1,0:T(8,128)S(1)} %fusion.66, f32[2,96,8,512]{3,2,1,0:T(8,128)S(1)} %copy-done.6, f32[2,96,8,512]{3,2,1,0:T(8,128)} %fusion.21, ...), kind=kOutput, calls=%fused_computation.44 | convolution fusion | flops 4844945408 | bytes 25198592 | tf_op jit(solution)/shard_map/...km,mj->...kj/dot_general | solution.py:59
  322.9 9.4 fusion.141
  332.4 9.6 fusion.143
  341.9 9.7 convolution_add_fusion.1
  351.7 9.4 convolution_subtract_fusion
  378.0 19.6 %all_to_all.75 = bf16[2,96,2048]{1,0,2:T(2,128)(2,1)} all-to-all(bf16[2,96,2048]{1,0,2:T(2,128)(2,1)} %copy.106), channel_id=1, replica_groups=mesh['dp'=4,'freq'=8] {'freq'}, dimensions={2} | all-to-all | bytes 1572864 | tf_op jit(solution)/shard_map/all_to_all | solution.py:244
  416.4 9.8 convolution_bitcast_fusion.2
  429.6 10.0 convolution_bitcast_fusion.1
  439.7 9.9 fusion.157
  449.6 7.3 fusion.159
  456.9 7.3 convolution_add_fusion.3
  464.3 7.5 convolution_subtract_fusion.2
  485.2 6.6 all-to-all-done.5
  529.7 31.7 %reduce-scatter.41.cloned.1.call-done = f32[768,384]{1,0:T(8,128)} async-done(((f32[768,3072]{1,0:T(8,128)}), f32[768,384]{1,0:T(8,128)}) %reduce-scatter.41.cloned.1.call-update) | async-done | bytes 1179664 | tf_op jit(solution)/shard_map/reduce_scatter | solution.py:279
  563.6 9.4 add_convert_fusion.2
  573.1 25.1 %reduce-scatter.59.cloned.1.call-done = f32[96,1]{1,0:T(8,128)} async-done(((f32[768,1]{1,0:T(8,128)}), f32[96,1]{1,0:T(8,128)}) %reduce-scatter.59.cloned.1.call-update) | async-done | bytes 400
  599.6 35.3 %reduce-scatter.61.cloned.1.call-done = f32[96,1]{1,0:T(8,128)} async-done(((f32[768,1]{1,0:T(8,128)}), f32[96,1]{1,0:T(8,128)}) %reduce-scatter.61.cloned.1.call-update) | async-done | bytes 400
  636.3 78.4 %reduce-scatter.45.cloned.1.call-done = f32[3072,96]{0,1:T(8,128)} async-done(((f32[3072,768]{0,1:T(8,128)}), f32[3072,96]{0,1:T(8,128)}) %reduce-scatter.45.cloned.1.call-update) | async-done | bytes 1179664 | tf_op jit(solution)/shard_map/reduce_scatter | solution.py:280
  716.9 34.7 %reduce-scatter.63.cloned.1.call-done = f32[96,1]{1,0:T(8,128)} async-done(((f32[768,1]{1,0:T(8,128)}), f32[96,1]{1,0:T(8,128)}) %reduce-scatter.63.cloned.1.call-update) | async-done | bytes 400
  757.0 36.4 %reduce-scatter.65.cloned.1.call-done = f32[384,1]{1,0:T(8,128)} async-done(((f32[3072,1]{1,0:T(8,128)}), f32[384,1]{1,0:T(8,128)}) %reduce-scatter.65.cloned.1.call-update) | async-done | bytes 1552
  796.2 34.1 %reduce-scatter.67.cloned.1.call-done = f32[96,1]{1,0:T(8,128)} async-done(((f32[768,1]{1,0:T(8,128)}), f32[96,1]{1,0:T(8,128)}) %reduce-scatter.67.cloned.1.call-update) | async-done | bytes 400
  833.0 34.0 %reduce-scatter.49.cloned.1.call-done = f32[96,1]{1,0:T(8,128)} async-done(((f32[768,1]{1,0:T(8,128)}), f32[96,1]{1,0:T(8,128)}) %reduce-scatter.49.cloned.1.call-update) | async-done | bytes 400
  869.8 34.2 %reduce-scatter.51.cloned.1.call-done = f32[96,1]{1,0:T(8,128)} async-done(((f32[768,1]{1,0:T(8,128)}), f32[96,1]{1,0:T(8,128)}) %reduce-scatter.51.cloned.1.call-update) | async-done | bytes 400
  906.7 37.2 %reduce-scatter.55.cloned.1.call-done = f32[288,1]{1,0:T(8,128)} async-done(((f32[2304,1]{1,0:T(8,128)}), f32[288,1]{1,0:T(8,128)}) %reduce-scatter.55.cloned.1.call-update) | async-done | bytes 1168
  944.9 12.6 %all-reduce = (bf16[96]{0:T(256)(128)(2,1)}, bf16[96]{0:T(256)(128)(2,1)}, bf16[288]{0:T(512)(128)(2,1)}, bf16[96]{0:T(256)(128)(2,1)}, bf16[96]{0:T(256)(128)(2...) all-reduce(bf16[96]{0:T(256)(128)(2,1)} %bitcast.318, ...), channel_id=1, replica_groups=mesh['dp'=4,'freq'=8] {'dp'}, use_global_device_ids=true, to_apply=%region_10.11 | all-reduce | flops 1344 | bytes 5376 | tf_op jit(solution)/shard_map/psum | solution.py:305
  972.5 15.9 %reduce-scatter.53.cloned.1.call-done = bf16[192,288]{1,0:T(8,128)(2,1)} async-done(((bf16[768,288]{1,0:T(8,128)(2,1)}), bf16[192,288]{1,0:T(8,128)(2,1)}) %reduce-scatter.53.cloned.1.call-update) | async-done | bytes 110608
  991.8 19.3 %reduce-scatter.43.cloned.1.call-done = bf16[192,384]{1,0:T(8,128)(2,1)} async-done(((bf16[768,384]{1,0:T(8,128)(2,1)}), bf16[192,384]{1,0:T(8,128)(2,1)}) %reduce-scatter.43.cloned.1.call-update) | async-done | bytes 147472 | tf_op jit(solution)/shard_map/reduce_scatter | solution.py:297
  1012.8 21.0 %reduce-scatter.47.cloned.1.call-done = bf16[768,96]{0,1:T(8,128)(2,1)} async-done(((bf16[3072,96]{0,1:T(8,128)(2,1)}), bf16[768,96]{0,1:T(8,128)(2,1)}) %reduce-scatter.47.cloned.1.call-update) | async-done | bytes 147472 | tf_op jit(solution)/shard_map/reduce_scatter | solution.py:300
  (343 shorter events, 249.6 us)
Async XLA Ops:
  8.0 10.3 copy-start
  8.0 8.7 copy-start.12
  8.0 10.2 copy-start.58
  8.1 10.2 copy-start.71
  11.1 12.8 %collective-permute-start = (bf16[768,1]{1,0:T(8,128)(2,1)}, bf16[768,1]{1,0:T(8,128)(2,1)}, u32[]{:S(2)}, u32[]{:S(2)}) collective-permute-start(bf16[768,1]{1,0:T(8,128)(2,1)} %get-tuple-element.110), channel_id=1, source_target_pairs={{0,1},{1,2},{2,3},{3,4},{4,5},{5,6},{6,7},{8,9},{9,10},{10,11},{11... | collective-permute-start | bytes 4616 | tf_op jit(solution)/shard_map/ppermute | solution.py:16
  14.1 9.8 collective-permute-start.1
  23.9 12.1 %copy-start.47 = (f32[2,256]{1,0:T(2,128)}, f32[2,256]{1,0:T(2,128)S(1)}, u32[]{:S(2)}) copy-start(f32[2,256]{1,0:T(2,128)S(1)} %compare_convert_fusion) | copy-start | bytes 6148
  26.6 14.9 %all-to-all-start.1 = ((bf16[8,96,256]{2,1,0:T(8,128)(2,1)}), bf16[8,96,256]{2,1,0:T(8,128)(2,1)}, u32[]{:S(2)}, u32[]{:S(2)}) async-start(bf16[8,96,256]{2,1,0:T(8,128)(2,1)} %bitcast.310), calls=%async_computation.1 | async-start | bytes 786432 | tf_op jit(solution)/shard_map/all_to_all | solution.py:120
  41.5 41.8 %all-to-all-start = ((bf16[2,768,256]{2,0,1:T(2,128)(2,1)}), bf16[2,768,256]{2,0,1:T(2,128)(2,1)}, u32[]{:S(2)}, u32[]{:S(2)}) async-start(bf16[2,768,256]{2,0,1:T(2,128)(2,1)} %copy.93), calls=%async_computation | async-start | bytes 1572864 | tf_op jit(solution)/shard_map/all_to_all | solution.py:142
  123.2 40.1 %copy-start.5 = (f32[2,96,8,512]{3,2,1,0:T(8,128)}, f32[2,96,8,512]{3,2,1,0:T(8,128)S(1)}, u32[]{:S(2)}) copy-start(f32[2,96,8,512]{3,2,1,0:T(8,128)S(1)} %fusion.57) | copy-start | bytes 9437188
  123.3 9.9 copy-start.1
  123.3 9.9 copy-start.3
  133.2 30.2 %copy-start.7 = (f32[2,96,8,512]{3,2,1,0:T(8,128)}, f32[2,96,8,512]{3,2,1,0:T(8,128)S(1)}, u32[]{:S(2)}) copy-start(f32[2,96,8,512]{3,2,1,0:T(8,128)S(1)} %fusion.60) | copy-start | bytes 9437188
  142.8 9.5 copy-start.17
  223.0 16.9 %copy-start.25 = (f32[2,256,768]{2,1,0:T(8,128)}, f32[2,256,768]{2,1,0:T(8,128)S(1)}, u32[]{:S(2)}) copy-start(f32[2,256,768]{2,1,0:T(8,128)S(1)} %get-tuple-element.113) | copy-start | bytes 4718596
  223.0 16.9 %copy-start.53 = (f32[2,256]{1,0:T(2,128)}, f32[2,256]{1,0:T(2,128)S(1)}, u32[]{:S(2)}) copy-start(f32[2,256]{1,0:T(2,128)S(1)} %broadcast_multiply_fusion) | copy-start | bytes 6148
  223.4 16.5 %copy-start.63 = (f32[2,256]{1,0:T(2,128)}, f32[2,256]{1,0:T(2,128)S(1)}, u32[]{:S(2)}) copy-start(f32[2,256]{1,0:T(2,128)S(1)} %fusion.235) | copy-start | bytes 6148
  223.4 12.9 %slice-start = ((s8[4718592]{0:T(1024)(128)(4,1)}), s8[4194304]{0:T(1024)(128)(4,1)S(1)}, s32[]{:S(2)}) async-start(s8[4718592]{0:T(1024)(128)(4,1)} %bitcast.320), calls=%async_computation.39 | async-start | bytes 8388608
  248.5 16.8 %all-to-all-start.3 = ((bf16[2,768,256]{2,0,1:T(2,128)(2,1)}), bf16[2,768,256]{2,0,1:T(2,128)(2,1)}, u32[]{:S(2)}, u32[]{:S(2)}) async-start(bf16[2,768,256]{2,0,1:T(2,128)(2,1)} %copy.102), calls=%async_computation.3 | async-start | bytes 1572864 | tf_op jit(solution)/shard_map/all_to_all | solution.py:216
  252.7 269.3 %reduce-scatter.39.cloned.1.call-start = ((), (), s32[]{:S(2)}) async-start(), calls=%async_computation.24 | async-start | bytes 2654208 | tf_op jit(solution)/shard_map/reduce_scatter | solution.py:278
  256.4 269.1 %reduce-scatter.37.cloned.1.call-start = ((), (), s32[]{:S(2)}) async-start(), calls=%async_computation.22 | async-start | bytes 7962624 | tf_op jit(solution)/shard_map/reduce_scatter | solution.py:277
  296.8 9.5 copy-start.6
  296.8 9.5 copy-start.8
  306.3 16.6 %copy-start.2 = (f32[96,8,512]{2,1,0:T(8,128)S(1)}, f32[96,8,512]{2,1,0:T(8,128)}, u32[]{:S(2)}) copy-start(f32[96,8,512]{2,1,0:T(8,128)} %fusion.103) | copy-start | bytes 4718596
  306.3 16.6 %copy-start.4 = (f32[96,8,512]{2,1,0:T(8,128)S(1)}, f32[96,8,512]{2,1,0:T(8,128)}, u32[]{:S(2)}) copy-start(f32[96,8,512]{2,1,0:T(8,128)} %fusion.106) | copy-start | bytes 4718596
  416.3 145.1 %reduce-scatter.41.cloned.1.call-start = ((), (), s32[]{:S(2)}) async-start(), calls=%async_computation.25 | async-start | bytes 10616832 | tf_op jit(solution)/shard_map/reduce_scatter | solution.py:279
  426.2 172.0 %reduce-scatter.59.cloned.1.call-start = ((), (), s32[]{:S(2)}) async-start(), calls=%async_computation.34 | async-start | bytes 442368
  427.9 207.0 %reduce-scatter.61.cloned.1.call-start = ((), (), s32[]{:S(2)}) async-start(), calls=%async_computation.35 | async-start | bytes 442368
  429.6 285.2 %reduce-scatter.45.cloned.1.call-start = ((), (), s32[]{:S(2)}) async-start(), calls=%async_computation.27 | async-start | bytes 10616832 | tf_op jit(solution)/shard_map/reduce_scatter | solution.py:280
  439.7 9.9 copy-start.41
  475.6 16.2 %copy-start.57 = (s32[768]{0:T(1024)S(1)}, s32[768]{0:T(1024)}, u32[]{:S(2)}) copy-start(s32[768]{0:T(1024)} %param.20) | copy-start | bytes 9220
  475.6 22.2 %copy-start.61 = (f32[3072]{0:T(1024)S(1)}, f32[3072]{0:T(1024)}, u32[]{:S(2)}) copy-start(f32[3072]{0:T(1024)} %get-tuple-element.116) | copy-start | bytes 36868
  479.3 12.5 %all-to-all-start.5 = ((bf16[96,8,256]{2,0,1:T(8,128)(2,1)}), bf16[96,8,256]{2,0,1:T(8,128)(2,1)}, u32[]{:S(2)}, u32[]{:S(2)}) async-start(bf16[96,8,256]{2,0,1:T(8,128)(2,1)} %copy.113), calls=%async_computation.6 | async-start | bytes 786432 | tf_op jit(solution)/shard_map/all_to_all | solution.py:231
  483.4 268.2 %reduce-scatter.63.cloned.1.call-start = ((), (), s32[]{:S(2)}) async-start(), calls=%async_computation.36 | async-start | bytes 442368
  485.1 308.3 %reduce-scatter.65.cloned.1.call-start = ((), (), s32[]{:S(2)}) async-start(), calls=%async_computation.37 | async-start | bytes 1769472
  494.6 5.1 collective-permute-start.2
  496.5 3.8 collective-permute-start.3
  499.5 330.8 %reduce-scatter.67.cloned.1.call-start = ((), (), s32[]{:S(2)}) async-start(), calls=%async_computation.38 | async-start | bytes 442368
  513.1 353.9 %reduce-scatter.49.cloned.1.call-start = ((), (), s32[]{:S(2)}) async-start(), calls=%async_computation.29 | async-start | bytes 442368
  515.1 388.9 %reduce-scatter.51.cloned.1.call-start = ((), (), s32[]{:S(2)}) async-start(), calls=%async_computation.30 | async-start | bytes 442368
  516.7 427.1 %reduce-scatter.55.cloned.1.call-start = ((), (), s32[]{:S(2)}) async-start(), calls=%async_computation.32 | async-start | bytes 1327104
  518.3 449.2 %all-reduce.3.cloned.1.call-start = ((), (), s32[]{:S(2)}) async-start(), calls=%async_computation.23 | async-start | bytes 786432 | tf_op jit(solution)/shard_map/psum | solution.py:313
  521.9 41.7 %copy-start.69 = (f32[3072]{0:T(1024)S(1)}, f32[3072]{0:T(1024)}, u32[]{:S(2)}) copy-start(f32[3072]{0:T(1024)} %param.32) | copy-start | bytes 36868
  521.9 41.7 %copy-start.74 = (f32[768]{0:T(1024)S(1)}, f32[768]{0:T(1024)}, u32[]{:S(2)}) copy-start(f32[768]{0:T(1024)} %param.34) | copy-start | bytes 9220
  521.9 447.5 %reduce-scatter.57.cloned.1.call-start = ((), (), s32[]{:S(2)}) async-start(), calls=%async_computation.33 | async-start | bytes 245760
  525.4 463.0 %reduce-scatter.53.cloned.1.call-start = ((), (), s32[]{:S(2)}) async-start(), calls=%async_computation.31 | async-start | bytes 737280
  529.6 481.6 %reduce-scatter.43.cloned.1.call-start = ((), (), s32[]{:S(2)}) async-start(), calls=%async_computation.26 | async-start | bytes 737280 | tf_op jit(solution)/shard_map/reduce_scatter | solution.py:297
  563.6 470.2 %reduce-scatter.47.cloned.1.call-start = ((), (), s32[]{:S(2)}) async-start(), calls=%async_computation.28 | async-start | bytes 737280 | tf_op jit(solution)/shard_map/reduce_scatter | solution.py:300
  (58 other events, 220.2 us)
Sparse Core Ops, SparseCore 0:
  256.9 44.0 reduce-scatter.38
  416.4 64.8 reduce-scatter.36
  484.8 76.4 reduce-scatter.40
  564.3 33.8 reduce-scatter.58
  601.1 33.7 reduce-scatter.60
  638.2 76.4 reduce-scatter.44
  717.8 33.8 reduce-scatter.62
  754.9 38.4 reduce-scatter.64
  796.5 33.7 reduce-scatter.66
  833.2 33.7 reduce-scatter.48
  870.1 33.7 reduce-scatter.50
  907.0 36.7 reduce-scatter.54
  946.7 19.3 reduce-scatter.56
  968.3 20.1 reduce-scatter.52
  990.6 20.4 reduce-scatter.42
  1013.4 20.3 reduce-scatter.46
Sparse Core Ops, SparseCore 1:
  522.0 40.9 all-reduce.2
where the time goes:
time: 1050 us; the launch traced here: 1040 us
  waiting for transfers between devices  456 us (43%)
  matrix products  322 us (31%)
  local copies, waits for them, and re-layouts  100 us (10%)
  other arithmetic  68 us (6%)
  blocking collectives  52 us (5%)
  starting transfers between devices  28 us (3%)
  between operations  17 us (2%)
    unnamed x27, waiting for transfers between devices  287 us
    reduce_scatter x1, waiting for transfers between devices, body(): lax.psum_scatter(down_projection_gradient, 'freq', scatter_dimension=1, t...  78.4 us
    unnamed x186, local copies, waits for them, and re-layouts  41.5 us
    dot_general x3, matrix products, forward_dft(): jnp.einsum('...km,mj->...kj', real_twist, inner_cos, precision=PRECISE)  34.2 us
    reduce_scatter x1, waiting for transfers between devices, body(): lax.psum_scatter(grad_fc_one, 'freq', scatter_dimension=1, tiled=True)  31.7 us
    dot_general x3, matrix products, inverse_dft(): jnp.einsum('...kj,jm->...km', imag_in, inner_cos, precision=PRECISE)  28.9 us
    dot_general x3, matrix products, forward_dft(): jnp.einsum('...km,mj->...kj', imag_twist, inner_sin, precision=PRECISE)  27.5 us
    dot_general x3, matrix products, forward_dft(): jnp.einsum('...km,mj->...kj', real_twist, inner_sin, precision=PRECISE)  27.1 us
  transfers between devices with their start and end apart: 25, of which 17 were waited for; matrix products, arithmetic and copies ran while one was open for 32% of the time, Pallas kernels for 0%

commit v1 on v0

v1 whole, which is shorter than its diff:
```python
import functools

import jax
import jax.numpy as jnp
import numpy as np
from jax import lax
from jax.experimental import pallas as pl
from jax.experimental.pallas import tpu as pltpu
from jax.sharding import PartitionSpec as P

NORM_EPS = 1e-05
SHRINK = 0.003
GELU_C = 0.7978845608028654
GELU_A = 0.044715
F32 = jnp.float32
BF16 = jnp.bfloat16
MIB = 1 << 20

NN = (((1,), (0,)), ((), ()))
NT = (((1,), (1,)), ((), ()))


def mm(left, right, dims=NN):
    return lax.dot_general(left, right, dims, preferred_element_type=F32)


def params(mib, grid_rank=0):
    kind = ("arbitrary",) * grid_rank if grid_rank else None
    return pltpu.CompilerParams(vmem_limit_bytes=mib * MIB, dimension_semantics=kind)


def vmem():
    return pl.BlockSpec(memory_space=pltpu.VMEM)


def smem():
    return pl.BlockSpec(memory_space=pltpu.SMEM)


def shape(dims, dtype):
    return jax.ShapeDtypeStruct(dims, dtype)


def cost(flops, moved, special=0):
    return pl.CostEstimate(flops=int(flops), bytes_accessed=int(moved), transcendentals=int(special))


def split16(table):
    high = np.asarray(table, np.float32).astype(jnp.bfloat16)
    low = (np.asarray(table, np.float64) - high.astype(np.float64)).astype(np.float32).astype(jnp.bfloat16)
    return high, low


@functools.lru_cache(maxsize=None)
def tables(width):
    order = np.concatenate([np.arange(0, width, 2), np.arange(1, width, 2)])
    turns = (2 * order[None, :] + 1) * np.arange(width)[:, None] % (4 * width)
    angle = np.pi * turns / (2 * width)
    forward = np.concatenate([np.cos(angle), -np.sin(angle)], axis=1)
    inverse = forward.T / width
    return split16(forward) + split16(inverse)


def split_value(value):
    high = value.astype(BF16)
    return high, (value - high.astype(F32)).astype(BF16)


def spectrum_of(block, fhi, flo):
    return mm(block, fhi) + mm(block, flo)


def signal_of(spec, ghi, glo):
    high, low = split_value(spec)
    return mm(high, ghi) + (mm(low, ghi) + mm(high, glo))


def each(count, step, unroll):
    if unroll:
        for i in range(count):
            step(i)
    else:
        lax.fori_loop(0, count, lambda i, c: (step(i), c)[1], 0)


def blocks_to_spectra(x_ref, spec_ref, fhi, flo, batch, width):
    count, chans = x_ref.shape[0], x_ref.shape[1]
    for b in range(batch):
        lanes = slice(b * width, (b + 1) * width)
        if chans % 16 == 0:
            rows = x_ref[:, :, lanes].reshape(count * chans, width)
            spec_ref[b] = spectrum_of(rows, fhi[...], flo[...]).reshape(count, chans, 2 * width)
        else:

            def step(j, b=b, lanes=lanes):
                spec_ref[b, j] = spectrum_of(x_ref[j, :, lanes], fhi[...], flo[...])

            each(count, step, False)


def tiles(chans, width, step):
    lane_tiles = width // 128

    def rows_step(rt):
        start = rt * 8 if isinstance(rt, int) else pl.multiple_of(rt * 8, 8)
        for lane in range(lane_tiles):
            step(pl.ds(start, 8), lane)

    each(chans // 8, rows_step, False)


def pair(ref, lead, rows, lane, width):
    return (
        ref[lead + (rows, slice(lane * 128, (lane + 1) * 128))],
        ref[lead + (rows, slice(width + lane * 128, width + (lane + 1) * 128))],
    )


def put_pair(ref, lead, rows, lane, width, value):
    ref[lead + (rows, slice(lane * 128, (lane + 1) * 128))] = value[0]
    ref[lead + (rows, slice(width + lane * 128, width + (lane + 1) * 128))] = value[1]


def times(a, k):
    return a[0] * k[0] - a[1] * k[1], a[0] * k[1] + a[1] * k[0]


def times_conj(a, k):
    return a[0] * k[0] + a[1] * k[1], a[1] * k[0] - a[0] * k[1]


def plus(a, b):
    return b if a is None else (a[0] + b[0], a[1] + b[1])


def quarter(now, before, sign):
    if before is None:
        return now
    if sign > 0:
        return now[0] - before[1], now[1] + before[0]
    return now[0] + before[1], now[1] - before[0]


def wide_quarter(now, before, width):
    lane = lax.broadcasted_iota(jnp.int32, (1, width), 1)
    sign = jnp.where(lane < width // 2, 1.0, -1.0)
    return jnp.concatenate(
        [now[:, :width] - sign * before[:, width:], now[:, width:] + sign * before[:, :width]], axis=1
    )


def wide_times(a, k, width, conj):
    ar, ai, kr, ki = a[:, :width], a[:, width:], k[:, :width], k[:, width:]
    if conj:
        return jnp.concatenate([ar * kr + ai * ki, ai * kr - ar * ki], axis=1)
    return jnp.concatenate([ar * kr - ai * ki, ar * ki + ai * kr], axis=1)


UNROLLED = 8


def small(count, chans, width):
    return count <= UNROLLED and chans % 16 == 0 and width % 256 == 0


def conv_products(spec_ref, k_ref, z_ref, batch, width, adjoint):
    reach, chans = k_ref.shape[0], k_ref.shape[1]
    count = spec_ref.shape[1]
    if small(count, chans, width):

        def step(rows, lane):
            k = [pair(k_ref, (d,), rows, lane, width) for d in range(reach)]
            for b in range(batch):
                x = [pair(spec_ref, (b, j), rows, lane, width) for j in range(count)]
                for i in range(count):
                    total = None
                    if adjoint:
                        for d in range(min(count - i, reach)):
                            total = plus(total, times_conj(x[i + d], k[d]))
                    else:
                        for d in range(min(i + 1, reach)):
                            total = plus(total, times(x[i - d], k[d]))
                    put_pair(z_ref, (b, i), rows, lane, width, total)

        tiles(chans, width, step)
        return
    for b in range(batch):

        def row(i, b=b):
            def term(d, total):
                src = i + d if adjoint else i - d
                return total + wide_times(spec_ref[b, src], k_ref[d], width, adjoint)

            terms = jnp.minimum(count - i if adjoint else i + 1, reach)
            z_ref[b, i] = lax.fori_loop(0, terms, term, jnp.zeros((chans, 2 * width), F32))

        each(count, row, False)


def conv_kernel(adjoint, x_ref, k_ref, skip_ref, fhi, flo, ghi, glo, out_ref, spec_ref, z_ref):
    count, chans, lanes = x_ref.shape
    width = fhi.shape[0]
    batch = lanes // width
    blocks_to_spectra(x_ref, spec_ref, fhi, flo, batch, width)
    conv_products(spec_ref, k_ref, z_ref, batch, width, adjoint)
    for b in range(batch):
        cut = slice(b * width, (b + 1) * width)
        if chans % 16 == 0:
            y = signal_of(z_ref[b].reshape(count * chans, 2 * width), ghi[...], glo[...])
            y = y.reshape(count, chans, width) + skip_ref[...][None] * x_ref[:, :, cut].astype(F32)
            out_ref[:, :, cut] = y.astype(BF16)
        else:

            def step(j, b=b, cut=cut):
                y = signal_of(z_ref[b, j], ghi[...], glo[...])
                out_ref[j, :, cut] = (y + skip_ref[...] * x_ref[j, :, cut].astype(F32)).astype(BF16)

            each(count, step, False)


def conv_call(x, k_spec, skip, adjoint):
    count, chans, lanes = x.shape
    width = k_spec.shape[2] // 2
    batch = lanes // width
    tabs = tables(width)
    spec = pltpu.VMEM((batch, count, chans, 2 * width), F32)
    return pl.pallas_call(
        functools.partial(conv_kernel, adjoint),
        out_shape=shape(x.shape, BF16),
        in_specs=[vmem()] * 7,
        out_specs=vmem(),
        scratch_shapes=[spec, spec],
        compiler_params=params(32),
        cost_estimate=cost(x.size * width * 20, x.size * 4 + k_spec.size * 4 + 4 * width * width * 4),
        name="conv_adjoint" if adjoint else "conv_forward",
    )(x, k_spec, skip, *tabs)


def pooled_rows(full):
    span = full.shape[1]
    place = lax.broadcasted_iota(jnp.int32, (1, span), 1)
    before = jnp.where(place == 0, 0.0, pltpu.roll(full, 1, 1))
    after = jnp.where(place == span - 1, 0.0, pltpu.roll(full, span - 1, 1))
    return (before + full + after) / 3.0


def taps_kernel(s_ref, len_ref, fhi, flo, out_ref, raw_ref):
    count, chans, width = s_ref.shape
    full = jnp.concatenate([s_ref[d].astype(F32) for d in range(count)], axis=1)
    place = lax.broadcasted_iota(jnp.int32, (1, count * width), 1)
    kernel = jnp.where(place < len_ref[...], pooled_rows(full), 0.0)
    for d in range(count):
        high, low = split_value(kernel[:, d * width : (d + 1) * width])
        raw_ref[d] = mm(high, fhi[...]) + (mm(low, fhi[...]) + mm(high, flo[...]))
    out_ref[0] = raw_ref[0]
    for d in range(1, count):
        out_ref[d] = wide_quarter(raw_ref[d], raw_ref[d - 1], width)
    if out_ref.shape[0] > count:
        out_ref[count] = wide_quarter(jnp.zeros((chans, 2 * width), F32), raw_ref[count - 1], width)


def taps_call(blocks, lens, token_blocks):
    count, chans, width = blocks.shape
    tabs = tables(width)
    return pl.pallas_call(
        taps_kernel,
        out_shape=shape((min(count + 1, token_blocks), chans, 2 * width), F32),
        in_specs=[vmem()] * 4,
        out_specs=vmem(),
        scratch_shapes=[pltpu.VMEM((count, chans, 2 * width), F32)],
        compiler_params=params(24),
        cost_estimate=cost(blocks.size * width * 12, blocks.size * 10),
        name="taps_spectra",
    )(blocks, lens, tabs[0], tabs[1])


def taps_grad_kernel(x_ref, g_ref, len_ref, fhi, flo, ghi, glo, out_ref, skip_ref, xs_ref, gs_ref, z_ref):
    count, chans, lanes = x_ref.shape
    reach = out_ref.shape[0]
    width = fhi.shape[0]
    batch = lanes // width
    blocks_to_spectra(x_ref, xs_ref, fhi, flo, batch, width)
    blocks_to_spectra(g_ref, gs_ref, fhi, flo, batch, width)
    if small(count, chans, width):

        def step(rows, lane):
            sign = 1 if lane < width // 256 else -1
            total = [None] * reach
            for b in range(batch):
                x = [pair(xs_ref, (b, j), rows, lane, width) for j in range(count)]
                x = [quarter(x[j], x[j - 1] if j else None, sign) for j in range(count)]
                for i in range(count):
                    g = pair(gs_ref, (b, i), rows, lane, width)
                    for d in range(min(i + 1, reach)):
                        total[d] = plus(total[d], times_conj(g, x[i - d]))
            for d in range(reach):
                put_pair(z_ref, (d,), rows, lane, width, total[d])

        tiles(chans, width, step)
        rows = signal_of(z_ref[...].reshape(reach * chans, 2 * width), ghi[...], glo[...])
        rows = rows.reshape(reach, chans, width)
        pieces = [rows[d] for d in range(reach)]
    else:

        def shift(t, c):
            j = count - 1 - t
            for b in range(batch):
                xs_ref[b, j] = wide_quarter(xs_ref[b, j], xs_ref[b, j - 1], width)
            return c

        lax.fori_loop(0, count - 1, shift, 0)

        def lag(d):
            total = jnp.zeros((chans, 2 * width), F32)
            for b in range(batch):

                def term(i, acc, b=b):
                    return acc + wide_times(gs_ref[b, i], xs_ref[b, i - d], width, True)

                total = lax.fori_loop(d, count, term, total)
            z_ref[d] = total

        each(reach, lag, False)
        pieces = [signal_of(z_ref[d], ghi[...], glo[...]) for d in range(reach)]
    full = jnp.concatenate(pieces, axis=1)
    place = lax.broadcasted_iota(jnp.int32, (1, reach * width), 1)
    full = pooled_rows(jnp.where(place < len_ref[...], full, 0.0))
    for d in range(reach):
        out_ref[d] = full[:, d * width : (d + 1) * width].astype(BF16)
    dot = jnp.zeros((chans, lanes), F32)
    for j in range(count):
        dot = dot + x_ref[j].astype(F32) * g_ref[j].astype(F32)
    skip_ref[...] = jnp.sum(dot, axis=1, keepdims=True)


def taps_grad_call(x, g, lens, width, reach):
    count, chans, lanes = x.shape
    batch = lanes // width
    tabs = tables(width)
    spec = pltpu.VMEM((batch, count, chans, 2 * width), F32)
    return pl.pallas_call(
        taps_grad_kernel,
        out_shape=(shape((reach, chans, width), BF16), shape((chans, 1), F32)),
        in_specs=[vmem()] * 7,
        out_specs=(vmem(), vmem()),
        scratch_shapes=[spec, spec, pltpu.VMEM((reach, chans, 2 * width), F32)],
        compiler_params=params(32),
        cost_estimate=cost(x.size * width * 20, x.size * 6),
        name="taps_gradient",
    )(x, g, lens, *tabs)


def normalized(values):
    centred = values - jnp.mean(values, axis=-1, keepdims=True)
    rate = lax.rsqrt(jnp.mean(centred * centred, axis=-1, keepdims=True) + NORM_EPS)
    return centred * rate, rate


def live_rows(offs_ref, batch, tok_rows, rows):
    row = lax.broadcasted_iota(jnp.int32, (rows, 1), 0)
    limit = jnp.zeros((rows, 1), jnp.int32)
    base = lax.axis_index("freq") * tok_rows
    position = base + row
    for b in range(batch):
        inside = jnp.logical_and(row >= b * tok_rows, row < (b + 1) * tok_rows)
        limit = jnp.where(inside, offs_ref[b] + b * tok_rows, limit)
    return position >= limit


def front_kernel(batch, tok_rows, offs_ref, tok, gain, bias, wv, wg, ws, bv, bg, bs, normed, mixed, value, gate, second):
    rows = tok.shape[0]

    @pl.when(pl.program_id(0) == 0)
    def _():
        n, _ = normalized(tok[...].astype(F32))
        normed[...] = (n * gain[...] + bias[...]).astype(BF16)

    x = normed[...]
    v = mm(x, wv[...]) + bv[...]
    g = mm(x, wg[...]) + bg[...]
    live = live_rows(offs_ref, batch, tok_rows, rows)
    mixed[...] = jnp.where(live, g * v, 0.0).T.astype(BF16)
    value[...] = jnp.where(live, v, 0.0).astype(BF16)
    gate[...] = jnp.where(live, g, 0.0).astype(BF16)
    second[...] = (mm(x, ws[...]) + bs[...]).astype(BF16)


def front_call(tok, offsets, gain, bias, weight, in_bias, batch, tok_rows):
    rows, width = tok.shape
    cut = 256
    per = width // cut

    def full(i):
        return (0, 0)

    def col(part):
        return lambda i: (0, part * per + i)

    act = shape((rows, width), BF16)
    return pl.pallas_call(
        functools.partial(front_kernel, batch, tok_rows),
        grid=(per,),
        out_shape=(act, shape((width, rows), BF16), act, act, act),
        in_specs=[smem(), pl.BlockSpec((rows, width), full), pl.BlockSpec((1, width), full), pl.BlockSpec((1, width), full)]
        + [pl.BlockSpec((width, cut), col(k)) for k in range(3)]
        + [pl.BlockSpec((1, cut), col(k)) for k in range(3)],
        out_specs=(
            pl.BlockSpec((rows, width), full),
            pl.BlockSpec((cut, rows), lambda i: (i, 0)),
            pl.BlockSpec((rows, cut), lambda i: (0, i)),
            pl.BlockSpec((rows, cut), lambda i: (0, i)),
            pl.BlockSpec((rows, cut), lambda i: (0, i)),
        ),
        compiler_params=params(32, 1),
        cost_estimate=cost(2 * rows * width * 3 * width, weight.size * 2 + rows * width * 12),
        name="norm_project",
    )(offsets, tok, gain, bias, weight, weight, weight, in_bias, in_bias, in_bias)


def gelu_parts(h):
    square = h * h
    t = jnp.tanh(GELU_C * h * (1.0 + GELU_A * square))
    half = 0.5 + 0.5 * t
    slope = half + (0.5 * GELU_C) * h * (1.0 - t * t) * (1.0 + (3.0 * GELU_A) * square)
    return h * half, slope


def mlp_kernel(paired, tok, convt, second, wo, ob, gain, bias, wup, b1, wdown, cot, *outs):
    gated, conv, res, n2t, act = outs[:5]
    hidden_outs, b1g, n2 = outs[5:-2], outs[-2], outs[-1]

    @pl.when(pl.program_id(0) == 0)
    def _():
        c = convt[...].astype(F32).T
        conv[...] = c.astype(BF16)
        g = (second[...].astype(F32) * c).astype(BF16)
        gated[...] = g
        r = tok[...].astype(F32) + (mm(g, wo[...]) + ob[...])
        res[...] = r
        n, _ = normalized(r)
        m = n * gain[...] + bias[...]
        n2[...] = m.astype(BF16)
        n2t[...] = m.T.astype(BF16)

    h = mm(n2[...], wup[...]) + b1[...]
    ag = mm(cot[...], wdown[...], NT)
    a, slope = gelu_parts(h)
    act[...] = a.astype(BF16)
    hg = (ag * slope).astype(BF16)
    b1g[...] = jnp.sum(hg.astype(F32), axis=0, keepdims=True)
    if not paired:
        hidden_outs[0][...] = hg
        return
    half = hg.shape[1] // 2
    mine, other = hidden_outs
    core = lax.rem(lax.axis_index("freq"), 2)

    @pl.when(core == 0)
    def _():
        mine[...] = hg[:, :half]
        other[...] = hg[:, half:]

    @pl.when(core == 1)
    def _():
        mine[...] = hg[:, half:]
        other[...] = hg[:, :half]


def mlp_call(tok, convt, second, wo, ob, gain, bias, wup, b1, wdown, cot, cut, paired):
    rows, width = tok.shape
    ff = wup.shape[1]

    def full(i):
        return (0, 0)

    def along(i):
        return (0, i)

    token = pl.BlockSpec((rows, width), full)
    vec = pl.BlockSpec((1, width), full)
    act = shape((rows, width), BF16)
    hidden = [shape((rows, ff // 2), BF16)] * 2 if paired else [shape((rows, ff), BF16)]
    hcut = cut // 2 if paired else cut
    return pl.pallas_call(
        functools.partial(mlp_kernel, paired),
        grid=(ff // cut,),
        out_shape=(act, act, shape((rows, width), F32), shape((width, rows), BF16), shape((rows, ff), BF16), *hidden, shape((1, ff), F32)),
        in_specs=[
            token,
            pl.BlockSpec((width, rows), full),
            token,
            pl.BlockSpec((width, width), full),
            vec,
            vec,
            vec,
            pl.BlockSpec((width, cut), along),
            pl.BlockSpec((1, cut), along),
            pl.BlockSpec((cut, width), lambda i: (i, 0)),
            token,
        ],
        out_specs=(
            token,
            token,
            token,
            pl.BlockSpec((width, rows), full),
            pl.BlockSpec((rows, cut), along),
            *[pl.BlockSpec((rows, hcut), along) for _ in hidden],
            pl.BlockSpec((1, cut), along),
        ),
        scratch_shapes=[pltpu.VMEM((rows, width), BF16)],
        compiler_params=params(48, 1),
        cost_estimate=cost(2 * rows * width * (2 * ff + width), wup.size * 4 + rows * ff * 4 + rows * width * 14, rows * ff),
        name="mix_out_mlp",
    )(tok, convt, second, wo, ob, gain, bias, wup, b1, wdown, cot)


def mlp_back_kernel(paired, freq_parts, *refs):
    hidden, rest = refs[: 2 if paired else 1], refs[2 if paired else 1 :]
    wup, res, gain, cot, wo, second, conv = rest[:7]
    rgrad, convgt, sgrad, brt_mine, brt_other, sgt_mine, sgt_other, vecs, acc = rest[7:]
    step = pl.program_id(0)
    core = lax.rem(lax.axis_index("freq"), 2)
    if paired:
        first = jnp.where(core == 0, hidden[0][...], hidden[1][...])
        later = jnp.where(core == 0, hidden[1][...], hidden[0][...])
        hg = jnp.concatenate([first, later], axis=1)
    else:
        hg = hidden[0][...]
    part = mm(hg, wup[...], NT)

    @pl.when(step == 0)
    def _():
        acc[...] = part

    @pl.when(step > 0)
    def _():
        acc[...] += part

    @pl.when(step == pl.num_programs(0) - 1)
    def _():
        ng = acc[...]
        n, rate = normalized(res[...])
        e = ng * gain[...]
        pulled = e - jnp.mean(e, axis=-1, keepdims=True) - n * jnp.mean(e * n, axis=-1, keepdims=True)
        r = cot[...].astype(F32) + rate * pulled
        rgrad[...] = r
        br = r.astype(BF16)
        brf = br.astype(F32)
        gg = mm(br, wo[...], NT)
        convgt[...] = (gg * second[...].astype(F32)).T.astype(BF16)
        sg = (gg * conv[...].astype(F32)).astype(BF16)
        sgrad[...] = sg
        sgf = sg.astype(F32)
        vecs[0:1] = jnp.sum(ng * n, axis=0, keepdims=True)
        vecs[1:2] = jnp.sum(ng, axis=0, keepdims=True)
        vecs[2:3] = jnp.sum(brf, axis=0, keepdims=True)
        vecs[3:4] = jnp.sum(sgf, axis=0, keepdims=True)
        put_halves(brf.T.astype(BF16), brt_mine, brt_other, core, freq_parts)
        put_halves(sgf.T.astype(BF16), sgt_mine, sgt_other, core, freq_parts)


def put_halves(value, mine, other, core, freq_parts):
    per = value.shape[0] // freq_parts
    even = [value[(2 * k) * per : (2 * k + 1) * per] for k in range(freq_parts // 2)]
    odd = [value[(2 * k + 1) * per : (2 * k + 2) * per] for k in range(freq_parts // 2)]

    def put(ref, blocks):
        for k, block in enumerate(blocks):
            ref[k * per : (k + 1) * per] = block

    @pl.when(core == 0)
    def _():
        put(mine, even)
        put(other, odd)

    @pl.when(core == 1)
    def _():
        put(mine, odd)
        put(other, even)


def mlp_back_call(hidden, wup, res, gain, cot, wo, second, conv, cut, paired, freq_parts):
    rows, width = res.shape
    ff = wup.shape[1]

    def full(i):
        return (0, 0)

    def along(i):
        return (0, i)

    token = pl.BlockSpec((rows, width), full)
    half = shape((width // 2, rows), BF16)
    half_spec = pl.BlockSpec((width // 2, rows), full)
    hcut = cut // 2 if paired else cut
    return pl.pallas_call(
        functools.partial(mlp_back_kernel, paired, freq_parts),
        grid=(ff // cut,),
        out_shape=(shape((rows, width), F32), shape((width, rows), BF16), shape((rows, width), BF16), half, half, half, half, shape((8, width), F32)),
        in_specs=[pl.BlockSpec((rows, hcut), along) for _ in hidden]
        + [pl.BlockSpec((width, cut), along), token, pl.BlockSpec((1, width), full), token, pl.BlockSpec((width, width), full), token, token],
        out_specs=(token, pl.BlockSpec((width, rows), full), token, half_spec, half_spec, half_spec, half_spec, pl.BlockSpec((8, width), full)),
        scratch_shapes=[pltpu.VMEM((rows, width), F32)],
        compiler_params=params(40, 1),
        cost_estimate=cost(2 * rows * width * (ff + width), wup.size * 2 + rows * ff * 2 + rows * width * 20),
        name="mlp_back",
    )(*hidden, wup, res, gain, cot, wo, second, conv)


def block_out_kernel(act, wdown, res, b2, cot, out, b2g, acc):
    step = pl.program_id(0)
    part = mm(act[...], wdown[...])

    @pl.when(step == 0)
    def _():
        acc[...] = res[...] + b2[...] + part
        b2g[...] = jnp.sum(cot[...].astype(F32), axis=0, keepdims=True)

    @pl.when(step > 0)
    def _():
        acc[...] += part

    @pl.when(step == pl.num_programs(0) - 1)
    def _():
        out[...] = acc[...].astype(BF16)


def block_out_call(act, wdown, res, b2, cot, cut):
    rows, width = res.shape
    ff = act.shape[1]

    def full(i):
        return (0, 0)

    token = pl.BlockSpec((rows, width), full)
    vec = pl.BlockSpec((1, width), full)
    return pl.pallas_call(
        block_out_kernel,
        grid=(ff // cut,),
        out_shape=(shape((rows, width), BF16), shape((1, width), F32)),
        in_specs=[pl.BlockSpec((rows, cut), lambda i: (0, i)), pl.BlockSpec((cut, width), lambda i: (i, 0)), token, vec, token],
        out_specs=(token, vec),
        scratch_shapes=[pltpu.VMEM((rows, width), F32)],
        compiler_params=params(24, 1),
        cost_estimate=cost(2 * rows * width * ff, wdown.size * 2 + rows * ff * 2 + rows * width * 8),
        name="block_out",
    )(act, wdown, res, b2, cot)


def back_kernel(freq_parts, mgt, value, gate, sgrad, weight, tok, gain, rgrad, out, v_mine, v_other, g_mine, g_other, vecs, mg, acc):
    step = pl.program_id(0)
    core = lax.rem(lax.axis_index("freq"), 2)

    @pl.when(step == 0)
    def _():
        m = mgt[...].astype(F32).T
        mg[...] = m.astype(BF16)
        acc[...] = mm(sgrad[...], weight[...], NT)

    @pl.when(step == 1)
    def _():
        pv = (gate[...].astype(F32) * mg[...].astype(F32)).astype(BF16)
        acc[...] += mm(pv, weight[...], NT)
        pf = pv.astype(F32)
        vecs[2:3] = jnp.sum(pf, axis=0, keepdims=True)
        put_halves(pf.T.astype(BF16), v_mine, v_other, core, freq_parts)

    @pl.when(step == 2)
    def _():
        pg = (value[...].astype(F32) * mg[...].astype(F32)).astype(BF16)
        ng = acc[...] + mm(pg, weight[...], NT)
        pf = pg.astype(F32)
        vecs[3:4] = jnp.sum(pf, axis=0, keepdims=True)
        put_halves(pf.T.astype(BF16), g_mine, g_other, core, freq_parts)
        n, rate = normalized(tok[...].astype(F32))
        vecs[0:1] = jnp.sum(ng * n, axis=0, keepdims=True)
        vecs[1:2] = jnp.sum(ng, axis=0, keepdims=True)
        e = ng * gain[...]
        pulled = e - jnp.mean(e, axis=-1, keepdims=True) - n * jnp.mean(e * n, axis=-1, keepdims=True)
        out[...] = (rgrad[...] + rate * pulled).astype(BF16)


def back_call(mgt, value, gate, sgrad, weight, tok, gain, rgrad, freq_parts):
    rows, width = tok.shape

    def full(i):
        return (0, 0)

    token = pl.BlockSpec((rows, width), full)
    half = shape((width // 2, rows), BF16)
    half_spec = pl.BlockSpec((width // 2, rows), full)
    return pl.pallas_call(
        functools.partial(back_kernel, freq_parts),
        grid=(3,),
        out_shape=(shape((rows, width), BF16), half, half, half, half, shape((8, width), F32)),
        in_specs=[
            pl.BlockSpec((width, rows), full),
            token,
            token,
            token,
            pl.BlockSpec((width, width), lambda i: (0, lax.rem(i + 2, 3))),
            token,
            pl.BlockSpec((1, width), full),
            token,
        ],
        out_specs=(token, half_spec, half_spec, half_spec, half_spec, pl.BlockSpec((8, width), full)),
        scratch_shapes=[pltpu.VMEM((rows, width), BF16), pltpu.VMEM((rows, width), F32)],
        compiler_params=params(32, 1),
        cost_estimate=cost(2 * rows * width * width * 3, weight.size * 2 + rows * width * 16),
        name="project_back",
    )(mgt, value, gate, sgrad, weight, tok, gain, rgrad)


def bit_order(chips, low_first):
    bits = list(range(chips.bit_length() - 1))
    return bits if low_first else bits[::-1]


def place_of(rel, order):
    place = 0
    for level, bit in enumerate(order):
        digit = lax.shift_right_logical(rel, bit) & 1
        place = place + digit * (1 << (len(order) - 1 - level))
    return place


def store_slot(keep, send, place, index, block):
    half = keep.shape[0]

    @pl.when(place < half)
    def _():
        keep[(place,) + index] = block

    @pl.when(place >= half)
    def _():
        send[(place - half,) + index] = block


def rows_kernel(chips, per, order, count, *refs):
    ins, (keep, send) = refs[: 4 * count], refs[4 * count :]
    chip = lax.axis_index("freq") // 2
    for p in range(count):
        lt, rt, ltp, rtp = ins[4 * p : 4 * p + 4]
        total = (mm(lt[...], rt[...]) + mm(ltp[...], rtp[...])).astype(BF16)
        for k in range(chips):
            place = place_of(jnp.int32(k) ^ chip, order)
            store_slot(keep, send, place, (slice(p * per, (p + 1) * per), slice(None)), total[k * per : (k + 1) * per])


def rows_pair(problems, chips, low_first, cut):
    order = bit_order(chips, low_first)
    rows, inner = problems[0][0].shape
    width = problems[0][1].shape[1]
    per = rows // chips
    if per % 16 or chips < 2:
        blocks = []
        for lt, rt, ltp, rtp in problems:
            blocks.append((mm(lt, rt) + mm(ltp, rtp)).astype(BF16).reshape(chips, per, width))
        return halves_of(jnp.concatenate(blocks, axis=1), order)
    count = len(problems)
    out = shape((chips // 2, count * per, width), BF16)
    out_spec = pl.BlockSpec((chips // 2, count * per, cut), lambda i: (0, 0, i))
    left = pl.BlockSpec((rows, inner), lambda i: (0, 0))
    right = pl.BlockSpec((inner, cut), lambda i: (0, i))
    return pl.pallas_call(
        functools.partial(rows_kernel, chips, per, order, count),
        grid=(width // cut,),
        out_shape=(out, out),
        in_specs=[left, right, left, right] * count,
        out_specs=(out_spec, out_spec),
        compiler_params=params(32, 1),
        cost_estimate=cost(4 * count * rows * inner * width, count * (rows * inner + inner * width + rows * width) * 4),
        name="row_gradients",
    )(*[x for problem in problems for x in problem])


def halves_of(blocks, order):
    chips = blocks.shape[0]
    chip = lax.axis_index("freq") // 2
    picks = np.zeros(chips, np.int32)
    for rel in range(chips):
        place = sum(((rel >> bit) & 1) << (len(order) - 1 - level) for level, bit in enumerate(order))
        picks[place] = rel
    moved = jnp.take(blocks, jnp.asarray(picks) ^ chip, axis=0)
    return moved[: chips // 2], moved[chips // 2 :]


def cols_kernel(order, lt, rt, ltp, rtp, keep, send):
    chip = lax.axis_index("freq") // 2
    total = (mm(lt[...], rt[...]) + mm(ltp[...], rtp[...])).astype(BF16)
    store_slot(keep, send, place_of(pl.program_id(0) ^ chip, order), (), total)


def cols_pair(lt, rt, ltp, rtp, chips, low_first):
    order = bit_order(chips, low_first)
    rows, inner = lt.shape
    per = rt.shape[1] // chips
    if per % 128 or chips < 2:
        total = (mm(lt, rt) + mm(ltp, rtp)).astype(BF16)
        return halves_of(total.reshape(rows, chips, per).transpose(1, 0, 2), order)
    out = shape((chips // 2, rows, per), BF16)
    out_spec = pl.BlockSpec((chips // 2, rows, per), lambda i: (0, 0, 0))
    left = pl.BlockSpec((rows, inner), lambda i: (0, 0))
    right = pl.BlockSpec((inner, per), lambda i: (0, i))
    return pl.pallas_call(
        functools.partial(cols_kernel, order),
        grid=(chips,),
        out_shape=(out, out),
        in_specs=[left, right, left, right],
        out_specs=(out_spec, out_spec),
        compiler_params=params(32, 1),
        cost_estimate=cost(4 * rows * inner * rt.shape[1], (rows * inner + inner * rt.shape[1] * 2) * 4),
        name="column_gradients",
    )(lt, rt, ltp, rtp)


def flip(value, freq_parts, bit):
    return lax.ppermute(value, "freq", [(i, i ^ bit) for i in range(freq_parts)])


def halving(keep, send, freq_parts, low_first):
    order = bit_order(freq_parts // 2, low_first)
    for level, bit in enumerate(order):
        got = flip(send, freq_parts, 2 << bit)
        total = keep.astype(F32) + got.astype(F32)
        if level == len(order) - 1:
            return total[0]
        half = total.shape[0] // 2
        keep, send = total[:half].astype(BF16), total[half:].astype(BF16)


def across(blocks):
    got = lax.all_to_all(blocks.astype(BF16), "dp", split_axis=0, concat_axis=0, tiled=True)
    return jnp.sum(got.astype(F32), axis=0)


def everywhere(rows):
    dp, freq = lax.axis_size("dp"), lax.axis_size("freq")
    wide = jnp.broadcast_to(rows[None], (dp,) + rows.shape).reshape(dp * freq, 1, rows.shape[1])
    got = lax.all_to_all(wide, ("dp", "freq"), split_axis=0, concat_axis=0, tiled=True)
    return jnp.sum(got, axis=(0, 1))


def reblocked(blocks, count, width):
    if blocks.shape[0] == count and blocks.shape[2] == width:
        return blocks
    whole = blocks.transpose(1, 0, 2).reshape(blocks.shape[1], -1)
    need = count * width
    whole = jnp.pad(whole, ((0, 0), (0, max(0, need - whole.shape[1]))))[:, :need]
    return whole.reshape(-1, count, width).transpose(1, 0, 2)


def body(tokens, offsets, kernel_lengths, norm1_gain, norm1_bias, w_in, in_bias, kernel_taps, skip_gain, w_out, out_bias, norm2_gain, norm2_bias, w_up, fc1_bias, w_down, fc2_bias, cotangent):
    freq = lax.axis_size("freq")
    dp = lax.axis_size("dp")
    chips = freq // 2
    batch, tok_rows, width = tokens.shape
    rows = batch * tok_rows
    ff = w_up.shape[1]
    chans = width // freq
    me = lax.axis_index("freq")
    core = lax.rem(me, 2)

    def row(v):
        return v.reshape(1, -1)

    tok = tokens.reshape(rows, width)
    cot = cotangent.reshape(rows, width)
    shrunk = (kernel_taps - SHRINK * jnp.tanh(kernel_taps / SHRINK)).astype(BF16)
    tap_rows = shrunk.shape[1]
    shrunk = lax.all_to_all(shrunk.reshape(freq, chans, tap_rows), "freq", split_axis=0, concat_axis=0, tiled=True)
    reach = -(-freq * tap_rows // tok_rows)
    shrunk = reblocked(shrunk, reach, tok_rows)
    lens = lax.dynamic_slice_in_dim(kernel_lengths, me * chans, chans).reshape(chans, 1)
    normed, mixed_t, value, gate, second = front_call(tok, offsets, row(norm1_gain), row(norm1_bias), w_in, row(in_bias), batch, tok_rows)
    mixed = lax.all_to_all(mixed_t.reshape(freq, chans, rows), "freq", split_axis=0, concat_axis=0, tiled=True)
    k_spec = taps_call(shrunk, lens, freq)
    skip = skip_gain.reshape(chans, 1)
    conv = conv_call(mixed, k_spec, skip, False)
    conv_t = lax.all_to_all(conv, "freq", split_axis=0, concat_axis=0, tiled=True).reshape(width, rows)
    cut = 768
    paired = (ff // freq) % 128 == 0 and 2 * (ff // freq) == cut
    outs = mlp_call(tok, conv_t, second, w_out, row(out_bias), row(norm2_gain), row(norm2_bias), w_up, row(fc1_bias), w_down, cot, cut, paired)
    gated, conv_tok, res, n2t, act = outs[:5]
    hidden, b1g = outs[5:-1], outs[-1]
    rgrad, convg_t, sgrad, br_mine, br_other, sg_mine, sg_other, vec_two = mlp_back_call(
        hidden, w_up, res, row(norm2_gain), cot, w_out, second, conv_tok, cut, paired, freq
    )
    convg = lax.all_to_all(convg_t.reshape(freq, chans, rows), "freq", split_axis=0, concat_axis=0, tiled=True)
    if paired:
        hg_mine, hg_other = hidden
    else:
        split = hidden[0].reshape(rows, chips, 2, ff // freq)
        hg_mine = jnp.take(split, core, axis=2).reshape(rows, ff // 2)
        hg_other = jnp.take(split, 1 - core, axis=2).reshape(rows, ff // 2)
    cot_t = cot.T.reshape(chips, 2, chans, rows)
    cot_mine = jnp.take(cot_t, core, axis=1).reshape(width // 2, rows)
    cot_other = jnp.take(cot_t, 1 - core, axis=1).reshape(width // 2, rows)

    def swap(v):
        return flip(v, freq, 1)

    normed_p, gated_p, n2t_p, act_p = swap(normed), swap(gated), swap(n2t), swap(act)
    fc2 = rows_pair([(cot_mine, act, swap(cot_other), act_p)], chips, True, 768)
    fc1 = cols_pair(n2t, hg_mine, n2t_p, swap(hg_other), chips, False)
    mixer = rows_pair([(br_mine, gated, swap(br_other), gated_p), (sg_mine, normed, swap(sg_other), normed_p)], chips, True, 384)
    block_out, b2g = block_out_call(act, w_down, res, row(fc2_bias), cot, cut)
    mixed_grad = conv_call(convg, k_spec, skip, True)
    mixed_grad_t = lax.all_to_all(mixed_grad, "freq", split_axis=0, concat_axis=0, tiled=True).reshape(width, rows)
    taps_g, skip_g = taps_grad_call(mixed, convg, lens, tok_rows, reach)
    taps_g = reblocked(taps_g, freq, tap_rows)
    taps_g = lax.all_to_all(taps_g, "freq", split_axis=0, concat_axis=0, tiled=True).reshape(width, tap_rows)
    taps_g = taps_g.astype(F32) * jnp.square(jnp.tanh(kernel_taps / SHRINK))
    taps_final = lax.psum(taps_g.astype(BF16), "dp").astype(F32)
    fc2 = halving(*fc2, freq, True)
    fc2_final = across(fc2.reshape(chans, dp, ff // dp).transpose(1, 0, 2)).T
    fc1 = halving(*fc1, freq, False)
    fc1_final = across(fc1.reshape(dp, width // dp, ff // freq))
    mixer = halving(*mixer, freq, True)
    input_grad, v_mine, v_other, g_mine, g_other, vec_one = back_call(mixed_grad_t, value, gate, sgrad, w_in, tok, row(norm1_gain), rgrad, freq)
    gates = rows_pair([(v_mine, normed, swap(v_other), normed_p), (g_mine, normed, swap(g_other), normed_p)], chips, False, 384)
    gates = halving(*gates, freq, False)
    split = jnp.concatenate([mixer, gates], axis=0).reshape(4 * chans, dp, width // dp).transpose(1, 0, 2)
    late = across(split)
    out_final = late[:chans].T
    parts = jnp.stack([late[2 * chans : 3 * chans], late[3 * chans :], late[chans : 2 * chans]]).astype(BF16)
    pieces = []
    for r in range(3):
        part = lax.rem((freq % 3) * (r - me + 3 * freq), 3)
        piece = lax.dynamic_index_in_dim(parts, part, 0, keepdims=False)
        pieces.append(lax.ppermute(piece, "freq", [((3 * d + r) % freq, d) for d in range(freq)]))
    in_final = jnp.concatenate(pieces, axis=0).T.astype(F32)
    early = everywhere(
        jnp.concatenate([b1g.reshape(freq, -1), b2g.reshape(freq, -1)] + [vec_two[k].reshape(freq, -1) for k in range(3)], axis=1)
    )
    own = (jnp.arange(freq, dtype=jnp.int32) == me).astype(F32)[:, None] * skip_g.reshape(1, chans)
    bias_in = jnp.concatenate([vec_one[2], vec_one[3], vec_two[3]]).reshape(freq, -1)
    final = everywhere(jnp.concatenate([vec_one[0].reshape(freq, -1), vec_one[1].reshape(freq, -1), bias_in, own], axis=1))
    fa = ff // freq
    n1g, n1b, inb, skg = final[:chans], final[chans : 2 * chans], final[2 * chans : 5 * chans], final[5 * chans :]
    b1f, b2f = early[:fa], early[fa : fa + chans]
    n2g, n2b, outb = (early[fa + k * chans : fa + (k + 1) * chans] for k in (1, 2, 3))
    return (
        block_out.reshape(tokens.shape),
        input_grad.reshape(tokens.shape),
        n1g,
        n1b,
        in_final,
        inb,
        taps_final,
        skg,
        out_final,
        outb,
        n2g,
        n2b,
        fc1_final,
        b1f,
        fc2_final,
        b2f,
    )


def solution(mesh):
    token, whole, lead = P("dp", "freq", None), P(), P("freq")
    both = P("dp", "freq")
    in_specs = (token, P("dp"), whole, whole, whole, whole, whole, P(None, "freq"), lead) + (whole,) * 8 + (token,)
    out_specs = (token, token, lead, lead, both, lead, P(None, "freq"), lead, both, lead, lead, lead, both, lead, both, lead)
    return jax.shard_map(body, mesh=mesh, in_specs=in_specs, out_specs=out_specs, check_vma=False)
```

time: 1050 us -> 330 us (0.31)
  waiting for transfers between devices: 456 us -> 80.5 us
  matrix products: 322 us -> 0 us
  Pallas kernels: 0 us -> 78.5 us
  blocking collectives: 52 us -> 0 us
  other arithmetic: 68 us -> 24.5 us
  starting transfers between devices: 28 us -> 66.8 us
  local copies, waits for them, and re-layouts: 100 us -> 62.3 us
    dot_general x48 -> x0, matrix products: 322 us -> none  [the longest x3 34.2 us: forward_dft(): jnp.einsum('...km,mj->...kj', real_twist, inner_cos, precision=PRECISE)]
    unnamed x27 -> x1, waiting for transfers between devices: 287 us -> 0.02 us
    reduce_scatter x6 -> x0, waiting for transfers between devices: 150 us -> none  [the longest x1 78.4 us: body(): lax.psum_scatter(down_projection_gradient, 'freq', scatter_dimension=1, t...]
    pallas_call x0 -> x13, Pallas kernels: none -> 78.5 us  [the longest x3 14.5 us: rows_pair(): pl.pallas_call(functools.partial(rows_kernel, chips, per, order, count),...]
    all_to_all x2 -> x0, blocking collectives: 39.4 us -> none  [the longest x1 19.8 us: body(): lax.all_to_all(conv_chan, 'freq', split_axis=2, concat_axis=1, tiled=True)]
    ppermute x4 -> x21, waiting for transfers between devices: 0.72 us -> 32.9 us  [the longest x18 31.8 us: flip(): lax.ppermute(value, 'freq', [(i, i ^ bit) for i in range(freq_parts)])]
    all_to_all x4 -> x11, starting transfers between devices: 19.5 us -> 51 us  [the longest x3 13.3 us: across(): lax.all_to_all(blocks.astype(BF16), 'dp', split_axis=0, concat_axis=0, ti...]
    all_to_all x4 -> x11, waiting for transfers between devices: 17.3 us -> 44.8 us  [the longest x3 13.3 us: across(): lax.all_to_all(blocks.astype(BF16), 'dp', split_axis=0, concat_axis=0, ti...]
  transfers between devices with their start and end apart: 25 -> 33, of which waited for: 17 -> 10; matrix products, arithmetic and copies ran while one was open for 32% -> 11% of each run, Pallas kernels for 0% -> 16%
where the time goes in v1:
time: 330 us; the launch traced here: 327 us
  waiting for transfers between devices  80.5 us (24%)
  Pallas kernels  78.5 us (24%)
  starting transfers between devices  66.8 us (20%)
  local copies, waits for them, and re-layouts  62.3 us (19%)
  other arithmetic  24.5 us (7%)
  between operations  14.8 us (4%)
    unnamed x171, local copies, waits for them, and re-layouts  50.4 us
    ppermute x18, waiting for transfers between devices, flip(): lax.ppermute(value, 'freq', [(i, i ^ bit) for i in range(freq_parts)])  31.8 us
    pallas_call x3, Pallas kernels, rows_pair(): pl.pallas_call(functools.partial(rows_kernel, chips, per, order, count),...  14.5 us
    all_to_all x3, starting transfers between devices, across(): lax.all_to_all(blocks.astype(BF16), 'dp', split_axis=0, concat_axis=0, ti...  13.3 us
    all_to_all x3, waiting for transfers between devices, across(): lax.all_to_all(blocks.astype(BF16), 'dp', split_axis=0, concat_axis=0, ti...  13.3 us
    pallas_call x1, Pallas kernels, mlp_call(): pl.pallas_call(functools.partial(mlp_kernel, paired), grid=(ff // cut,),...  13.2 us
    all_to_all x1, waiting for transfers between devices, body(): lax.all_to_all(conv, 'freq', split_axis=0, concat_axis=0, tiled=True)  12.4 us
    all_to_all x1, waiting for transfers between devices, body(): lax.all_to_all(convg_t.reshape(freq, chans, rows), 'freq', split_axis=0,...  12.1 us
  transfers between devices with their start and end apart: 33, of which 10 were waited for; matrix products, arithmetic and copies ran while one was open for 11% of the time, Pallas kernels for 16%

profile of v1, /device:TPU:0, one launch (start us, length us, event | category | flops | bytes accessed | tf_op | source)
XLA Modules:
  0.0 327.5 jit_solution(14486288466401013741)
XLA Ops:
  7.2 2.1 subtract_convert_fusion
  9.3 5.2 %all-to-all-start.1 = ((bf16[8,96,256]{2,1,0:T(8,128)(2,1)}), bf16[8,96,256]{2,1,0:T(8,128)(2,1)S(1)}, u32[]{:S(2)}, u32[]{:S(2)}) async-start(bf16[8,96,256]{2,1,0:T(8,128)(2,1)} %bitcast.2), calls=%async_computation.1 | async-start | bytes 786432 | tf_op jit(solution)/shard_map/all_to_all | solution.py:871
  14.6 2.0 copy-done.2
  16.6 4.8 %norm_project.1 = (bf16[512,768]{1,0:T(8,128)(2,1)S(1)}, bf16[768,512]{1,0:T(8,128)(2,1)}, bf16[512,768]{1,0:T(8,128)(2,1)S(1)}, bf16[512,768]{1,0:T(8,128)(2,1)S(1)}, bf16[512,768]{1,0:T(8,128)(2,1)S(1)}) custom-call(s32[2]{0:T(128)S(1)} %copy-done.60, bf16[512,768]{1,0:T(8,128)(2,1)S(1)} %bitcast.54, f32[1,768]{1,0:T(1,128)S(1)} %reshape.138.gain, ...), custom_call_target="tpu_custom_call" | custom-call | flops 1811939328 | bytes 8257536 | tf_op jit(solution)/shard_map/norm_project/pallas_call | solution.py:400
  24.1 4.3 %all-to-all-start = ((bf16[8,96,512]{2,1,0:T(8,128)(2,1)}), bf16[8,96,512]{2,1,0:T(8,128)(2,1)}, u32[]{:S(2)}, u32[]{:S(2)}) async-start(bf16[8,96,512]{2,1,0:T(8,128)(2,1)} %bitcast.1), calls=%async_computation | async-start | bytes 1572864 | tf_op jit(solution)/shard_map/all_to_all | solution.py:876
  32.7 1.5 taps_spectra.1.k_ref
  34.1 7.0 %all-to-all-done.x_ref = bf16[8,96,512]{2,1,0:T(8,128)(2,1)} async-done(((bf16[8,96,512]{2,1,0:T(8,128)(2,1)}), bf16[8,96,512]{2,1,0:T(8,128)(2,1)}, u32[]{:S(2)}, u32[]{:S(2)}) %all-to-all-start) | async-done | bytes 786464 | tf_op jit(solution)/shard_map/all_to_all | solution.py:876
  45.7 5.4 %conv_forward.1 = bf16[8,96,512]{2,1,0:T(8,128)(2,1)S(1)} custom-call(bf16[8,96,512]{2,1,0:T(8,128)(2,1)} %all-to-all-done.x_ref, f32[8,96,512]{2,1,0:T(8,128)S(1)} %taps_spectra.1.k_ref, f32[96,1]{1,0:T(8,128)S(1)} %copy-done.53, bf16[256,512]{1,0:T(8,128)(2,1)S(1)} %copy-done.43, bf16[256,512]{1,0:T(8,128)(2,1)S(1)} %copy-done.47, ...), custom_call_target="tpu_custom_call" | custom-call | flops 2013265920 | bytes 4194304 | tf_op jit(solution)/shard_map/conv_forward/pallas_call | solution.py:227
  53.1 4.5 %all-to-all-start.2 = ((bf16[8,96,512]{2,1,0:T(8,128)(2,1)}), bf16[8,96,512]{2,1,0:T(8,128)(2,1)}, u32[]{:S(2)}, u32[]{:S(2)}) async-start(bf16[8,96,512]{2,1,0:T(8,128)(2,1)} %copy-done.27), calls=%async_computation.2 | async-start | bytes 1572864 | tf_op jit(solution)/shard_map/all_to_all | solution.py:880
  57.7 12.4 %all-to-all-done.2 = bf16[8,96,512]{2,1,0:T(8,128)(2,1)} async-done(((bf16[8,96,512]{2,1,0:T(8,128)(2,1)}), bf16[8,96,512]{2,1,0:T(8,128)(2,1)}, u32[]{:S(2)}, u32[]{:S(2)}) %all-to-all-start.2) | async-done | bytes 786464 | tf_op jit(solution)/shard_map/all_to_all | solution.py:880
  70.1 13.2 %mix_out_mlp.1 = (bf16[512,768]{1,0:T(8,128)(2,1)S(1)}, bf16[512,768]{1,0:T(8,128)(2,1)S(1)}, f32[512,768]{1,0:T(8,128)}, bf16[768,512]{1,0:T(8,128)(2,1)S(1)}, ...) custom-call(bf16[512,768]{1,0:T(8,128)(2,1)S(1)} %bitcast.55, ...), custom_call_target="tpu_custom_call" | custom-call | flops 5435817984 | bytes 21233664 | tf_op jit(solution)/shard_map/mix_out_mlp/pallas_call | solution.py:484
  84.2 1.7 copy-done.5
  88.8 9.1 %mlp_back.1 = (f32[512,768]{1,0:T(8,128)S(1)}, bf16[768,512]{1,0:T(8,128)(2,1)S(1)}, bf16[512,768]{1,0:T(8,128)(2,1)S(1)}, bf16[384,512]{1,0:T(8,128)(2,1)S(1)},...) custom-call(bf16[512,1536]{1,0:T(8,128)(2,1)S(1)} %copy-done.13, ...), custom_call_target="tpu_custom_call" | custom-call | flops 3019898880 | bytes 15728640 | tf_op jit(solution)/shard_map/mlp_back/pallas_call | solution.py:596
  102.9 3.5 %all-to-all-start.3 = ((bf16[8,96,512]{2,1,0:T(8,128)(2,1)}), bf16[8,96,512]{2,1,0:T(8,128)(2,1)S(1)}, u32[]{:S(2)}, u32[]{:S(2)}) async-start(bf16[8,96,512]{2,1,0:T(8,128)(2,1)} %bitcast.57), calls=%async_computation.3 | async-start | bytes 1572864 | tf_op jit(solution)/shard_map/all_to_all | solution.py:889
  106.8 12.1 %all-to-all-done.3.x_ref.g_ref = bf16[8,96,512]{2,1,0:T(8,128)(2,1)S(1)} async-done(((bf16[8,96,512]{2,1,0:T(8,128)(2,1)}), bf16[8,96,512]{2,1,0:T(8,128)(2,1)S(1)}, u32[]{:S(2)}, u32[]{:S(2)}) %all-to-all-start.3) | async-done | bytes 786464 | tf_op jit(solution)/shard_map/all_to_all | solution.py:889
  125.0 4.2 %conv_adjoint.1 = bf16[8,96,512]{2,1,0:T(8,128)(2,1)S(1)} custom-call(bf16[8,96,512]{2,1,0:T(8,128)(2,1)S(1)} %all-to-all-done.3.x_ref.g_ref, f32[8,96,512]{2,1,0:T(8,128)S(1)} %copy-done.12, f32[96,1]{1,0:T(8,128)S(1)} %copy-done.54, bf16[256,512]{1,0:T(8,128)(2,1)S(1)} %copy-done.44, bf16[256,512]{1,0:T(8,128)(2,1)S(1)} %copy-done.48, ...), custom_call_target="tpu_custom_call" | custom-call | flops 2013265920 | bytes 4194304 | tf_op jit(solution)/shard_map/conv_adjoint/pallas_call | solution.py:227
  130.1 4.3 %all-to-all-start.4 = ((bf16[8,96,512]{2,1,0:T(8,128)(2,1)}), bf16[8,96,512]{2,1,0:T(8,128)(2,1)}, u32[]{:S(2)}, u32[]{:S(2)}) async-start(bf16[8,96,512]{2,1,0:T(8,128)(2,1)} %copy-done.25), calls=%async_computation.4 | async-start | bytes 1572864 | tf_op jit(solution)/shard_map/all_to_all | solution.py:909
  136.0 2.2 dynamic-slice_select_fusion
  138.9 2.3 copy-done.7
  141.2 1.9 copy-done.8
  143.1 5.2 %block_out.1 = (bf16[512,768]{1,0:T(8,128)(2,1)}, f32[1,768]{1,0:T(1,128)S(1)}) custom-call(bf16[512,3072]{1,0:T(8,128)(2,1)S(1)} %copy-done.8, bf16[3072,768]{1,0:T(8,128)(2,1)S(1)} %copy-done.7, f32[512,768]{1,0:T(8,128)S(1)} %copy-done.6, f32[1,768]{1,0:T(1,128)S(1)} %reshape.151.b2, bf16[512,768]{1,0:T(8,128)(2,1)S(1)} %bitcast.53), custom_call_target="tpu_custom_call" | custom-call | flops 2415919104 | bytes 11010048 | tf_op jit(solution)/shard_map/block_out/pallas_call | solution.py:637
  151.4 6.5 %all-to-all-start.8 = ((f32[32,1,768]{2,1,0:T(1,128)}), f32[32,1,768]{2,1,0:T(1,128)}, u32[]{:S(2)}, u32[]{:S(2)}) async-start(f32[32,1,768]{2,1,0:T(1,128)} %reshape.160), calls=%async_computation.8 | async-start | bytes 196608 | tf_op jit(solution)/shard_map/all_to_all | solution.py:840
  163.6 7.5 %taps_gradient.1 = (bf16[8,96,256]{2,1,0:T(8,128)(2,1)S(1)}, f32[96,1]{1,0:T(8,128)S(1)}) custom-call(bf16[8,96,512]{2,1,0:T(8,128)(2,1)} %all-to-all-done.x_ref, bf16[8,96,512]{2,1,0:T(8,128)(2,1)S(1)} %copy-done.24, s32[96,1]{1,0:T(8,128)S(1)} %copy-done.51, bf16[256,512]{1,0:T(8,128)(2,1)S(1)} %copy-done.45, bf16[256,512]{1,0:T(8,128)(2,1)S(1)} %copy-done.49, ...), custom_call_target="tpu_custom_call" | custom-call | flops 2013265920 | bytes 2359296 | tf_op jit(solution)/shard_map/taps_gradient/pallas_call | solution.py:341
  173.7 6.3 %project_back.1 = (bf16[512,768]{1,0:T(8,128)(2,1)}, bf16[384,512]{1,0:T(8,128)(2,1)S(1)}, bf16[384,512]{1,0:T(8,128)(2,1)S(1)}, bf16[384,512]{1,0:T(8,128)(2,1)...) custom-call(bf16[768,512]{1,0:T(8,128)(2,1)} %bitcast.10.mgt, bf16[512,768]{1,0:T(8,128)(2,1)S(1)} %copy-done.29, ...), custom_call_target="tpu_custom_call" | custom-call | flops 1811939328 | bytes 9830400 | tf_op jit(solution)/shard_map/project_back/pallas_call | solution.py:692
  182.9 4.2 %all-to-all-start.7 = ((bf16[8,96,256]{2,1,0:T(8,128)(2,1)}), bf16[8,96,256]{2,1,0:T(8,128)(2,1)}, u32[]{:S(2)}, u32[]{:S(2)}) async-start(bf16[8,96,256]{2,1,0:T(8,128)(2,1)} %copy-done.40), calls=%async_computation.7 | async-start | bytes 786432 | tf_op jit(solution)/shard_map/all_to_all | solution.py:912
  191.3 4.6 %row_gradients.3 = (bf16[2,192,768]{2,1,0:T(8,128)(2,1)S(1)}, bf16[2,192,768]{2,1,0:T(8,128)(2,1)}) custom-call(bf16[384,512]{1,0:T(8,128)(2,1)S(1)} %get-tuple-element.73.refs_0_, bf16[512,768]{1,0:T(8,128)(2,1)S(1)} %copy-done.20, bf16[384,512]{1,0:T(8,128)(2,1)} %collective-permute-done.refs_2_, bf16[512,768]{1,0:T(8,128)(2,1)} %collective-permute-done.1.refs_3_, ...), custom_call_target="tpu_custom_call" | custom-call | flops 1207959552 | bytes 7077888 | tf_op jit(solution)/shard_map/row_gradients/pallas_call | solution.py:765
  195.9 1.9 collective-permute-start.4
  197.8 2.2 fusion
  201.1 5.1 %all-to-all-start.5 = ((f32[32,1,576]{2,1,0:T(1,128)}), f32[32,1,576]{2,1,0:T(1,128)S(1)}, u32[]{:S(2)}, u32[]{:S(2)}) async-start(f32[32,1,576]{2,1,0:T(1,128)} %reshape.157), calls=%async_computation.5 | async-start | bytes 163840 | tf_op jit(solution)/shard_map/all_to_all | solution.py:840
  206.3 3.8 %row_gradients.4 = (bf16[2,192,768]{2,1,0:T(8,128)(2,1)S(1)}, bf16[2,192,768]{2,1,0:T(8,128)(2,1)S(1)}) custom-call(bf16[384,512]{1,0:T(8,128)(2,1)S(1)} %copy-done.37, bf16[512,768]{1,0:T(8,128)(2,1)S(1)} %get-tuple-element.77.refs_5_.refs_1_, bf16[384,512]{1,0:T(8,128)(2,1)} %collective-permute-done.6.refs_2_, ...), custom_call_target="tpu_custom_call" | custom-call | flops 1207959552 | bytes 7077888 | tf_op jit(solution)/shard_map/row_gradients/pallas_call | solution.py:765
  210.2 2.4 collective-permute-done.4
  212.5 1.6 collective-permute-start.8
  216.8 7.0 %column_gradients.1 = (bf16[2,768,384]{2,1,0:T(8,128)(2,1)S(1)}, bf16[2,768,384]{2,1,0:T(8,128)(2,1)}) custom-call(bf16[768,512]{1,0:T(8,128)(2,1)S(1)} %copy-done.62, bf16[512,1536]{1,0:T(8,128)(2,1)S(1)} %copy-done.14, bf16[768,512]{1,0:T(8,128)(2,1)} %collective-permute-done.13.ltp, bf16[512,1536]{1,0:T(8,128)(2,1)} %collective-permute-done.14.rtp), custom_call_target="tpu_custom_call" | custom-call | flops 2415919104 | bytes 7864320 | tf_op jit(solution)/shard_map/column_gradients/pallas_call | solution.py:805
  225.1 6.0 %row_gradients.5 = (bf16[2,96,3072]{2,1,0:T(8,128)(2,1)S(1)}, bf16[2,96,3072]{2,1,0:T(8,128)(2,1)}) custom-call(bf16[384,512]{1,0:T(8,128)(2,1)S(1)} %bitcast.58, bf16[512,3072]{1,0:T(8,128)(2,1)S(1)} %copy-done.9, bf16[384,512]{1,0:T(8,128)(2,1)S(1)} %collective-permute-done.17.refs_2_, bf16[512,3072]{1,0:T(8,128)(2,1)} %collective-permute-done.18.refs_3_), custom_call_target="tpu_custom_call" | custom-call | flops 2415919104 | bytes 11796480 | tf_op jit(solution)/shard_map/row_gradients/pallas_call | solution.py:765
  231.2 1.6 collective-permute-start.19
  236.1 2.9 all-reduce.2.cloned.1.call-done
  238.9 1.9 convert_element_type.130
  242.2 21.7 %collective-permute-done.9 = bf16[1,192,768]{2,1,0:T(8,128)(2,1)} collective-permute-done((bf16[1,192,768]{2,1,0:T(8,128)(2,1)}, bf16[1,192,768]{2,1,0:T(8,128)(2,1)}, u32[]{:S(2)}, u32[]{:S(2)}) %collective-permute-start.9) | collective-permute-done | bytes 294944 | tf_op jit(solution)/shard_map/ppermute | solution.py:818
  266.2 5.0 %all-to-all-start.6 = ((bf16[4,384,192]{1,2,0:T(8,128)(2,1)}), bf16[4,384,192]{1,2,0:T(8,128)(2,1)S(1)}, u32[]{:S(2)}, u32[]{:S(2)}) async-start(bf16[4,384,192]{1,2,0:T(8,128)(2,1)} %maximum_bitcast_fusion), calls=%async_computation.6 | async-start | bytes 1179648 | tf_op jit(solution)/shard_map/all_to_all | solution.py:833
  271.2 1.6 add_convert_fusion.1
  272.9 1.5 collective-permute-start.16
  274.5 1.7 add_convert_fusion
  277.7 7.7 %collective-permute-done.16 = bf16[1,768,384]{2,1,0:T(8,128)(2,1)S(1)} collective-permute-done((bf16[1,768,384]{2,1,0:T(8,128)(2,1)S(1)}, bf16[1,768,384]{2,1,0:T(8,128)(2,1)S(1)}, u32[]{:S(2)}, u32[]{:S(2)}) %collective-permute-start.16) | collective-permute-done | bytes 589856 | tf_op jit(solution)/shard_map/ppermute | solution.py:818
  286.3 4.8 %all-to-all-start.9 = ((bf16[4,192,384]{2,1,0:T(8,128)(2,1)}), bf16[4,192,384]{2,1,0:T(8,128)(2,1)S(1)}, u32[]{:S(2)}, u32[]{:S(2)}) async-start(bf16[4,192,384]{2,1,0:T(8,128)(2,1)} %bitcast.24), calls=%async_computation.9 | async-start | bytes 1179648 | tf_op jit(solution)/shard_map/all_to_all | solution.py:833
  295.3 8.0 %all-to-all-done.9 = bf16[4,192,384]{2,1,0:T(8,128)(2,1)S(1)} async-done(((bf16[4,192,384]{2,1,0:T(8,128)(2,1)}), bf16[4,192,384]{2,1,0:T(8,128)(2,1)S(1)}, u32[]{:S(2)}, u32[]{:S(2)}) %all-to-all-start.9) | async-done | bytes 589856 | tf_op jit(solution)/shard_map/all_to_all | solution.py:833
  303.3 3.5 %all-to-all-start.10 = ((bf16[4,96,768]{2,1,0:T(8,128)(2,1)}), bf16[4,96,768]{2,1,0:T(8,128)(2,1)S(1)}, u32[]{:S(2)}, u32[]{:S(2)}) async-start(bf16[4,96,768]{2,1,0:T(8,128)(2,1)} %bitcast.49), calls=%async_computation.10 | async-start | bytes 1179648 | tf_op jit(solution)/shard_map/all_to_all | solution.py:833
  306.9 3.4 %collective-permute-start.12 = (bf16[96,192]{1,0:T(8,128)(2,1)S(1)}, bf16[96,192]{1,0:T(8,128)(2,1)S(1)}, u32[]{:S(2)}, u32[]{:S(2)}) collective-permute-start(bf16[96,192]{1,0:T(8,128)(2,1)S(1)} %get-tuple-element.152), channel_id=1, source_target_pairs={{2,0},{5,1},{0,2},{3,3},{6,4},{1,5},{4,6},{7,7},{10,8},{13,9},{8,1... | collective-permute-start | bytes 110600 | tf_op jit(solution)/shard_map/ppermute | solution.py:931
  314.6 5.3 %all-to-all-done.10 = bf16[4,96,768]{2,1,0:T(8,128)(2,1)S(1)} async-done(((bf16[4,96,768]{2,1,0:T(8,128)(2,1)}), bf16[4,96,768]{2,1,0:T(8,128)(2,1)S(1)}, u32[]{:S(2)}, u32[]{:S(2)}) %all-to-all-start.10) | async-done | bytes 589856 | tf_op jit(solution)/shard_map/all_to_all | solution.py:833
  (273 shorter events, 74.2 us)
Async XLA Ops:
  7.2 21.3 %copy-start = (s32[768]{0:T(1024)S(1)}, s32[768]{0:T(1024)}, u32[]{:S(2)}) copy-start(s32[768]{0:T(1024)} %param.26) | copy-start | bytes 9220
  9.3 14.8 %all-to-all-start.1 = ((bf16[8,96,256]{2,1,0:T(8,128)(2,1)}), bf16[8,96,256]{2,1,0:T(8,128)(2,1)S(1)}, u32[]{:S(2)}, u32[]{:S(2)}) async-start(bf16[8,96,256]{2,1,0:T(8,128)(2,1)} %bitcast.2), calls=%async_computation.1 | async-start | bytes 786432 | tf_op jit(solution)/shard_map/all_to_all | solution.py:871
  24.1 17.0 %all-to-all-start = ((bf16[8,96,512]{2,1,0:T(8,128)(2,1)}), bf16[8,96,512]{2,1,0:T(8,128)(2,1)}, u32[]{:S(2)}, u32[]{:S(2)}) async-start(bf16[8,96,512]{2,1,0:T(8,128)(2,1)} %bitcast.1), calls=%async_computation | async-start | bytes 1572864 | tf_op jit(solution)/shard_map/all_to_all | solution.py:876
  45.7 12.0 %copy-start.79 = (f32[768]{0:T(1024)S(1)}, f32[768]{0:T(1024)}, u32[]{:S(2)}) copy-start(f32[768]{0:T(1024)} %param.34) | copy-start | bytes 9220
  45.7 12.0 %copy-start.80 = (f32[768]{0:T(1024)S(1)}, f32[768]{0:T(1024)}, u32[]{:S(2)}) copy-start(f32[768]{0:T(1024)} %param.35) | copy-start | bytes 9220
  45.7 12.0 %copy-start.81 = (f32[768]{0:T(1024)S(1)}, f32[768]{0:T(1024)}, u32[]{:S(2)}) copy-start(f32[768]{0:T(1024)} %param.36) | copy-start | bytes 9220
  53.1 17.0 %copy-start.4 = (bf16[2,256,768]{2,1,0:T(8,128)(2,1)S(1)}, bf16[2,256,768]{2,1,0:T(8,128)(2,1)}, u32[]{:S(2)}) copy-start(bf16[2,256,768]{2,1,0:T(8,128)(2,1)} %param.41) | copy-start | bytes 2359300
  53.1 17.0 %copy-start.22 = (bf16[512,768]{1,0:T(8,128)(2,1)S(1)}, bf16[512,768]{1,0:T(8,128)(2,1)}, u32[]{:S(2)}) copy-start(bf16[512,768]{1,0:T(8,128)(2,1)} %copy-done.21) | copy-start | bytes 2359300
  53.1 17.0 %copy-start.65 = (f32[3072]{0:T(1024)S(1)}, f32[3072]{0:T(1024)}, u32[]{:S(2)}) copy-start(f32[3072]{0:T(1024)} %param.38) | copy-start | bytes 36868
  53.1 17.0 %all-to-all-start.2 = ((bf16[8,96,512]{2,1,0:T(8,128)(2,1)}), bf16[8,96,512]{2,1,0:T(8,128)(2,1)}, u32[]{:S(2)}, u32[]{:S(2)}) async-start(bf16[8,96,512]{2,1,0:T(8,128)(2,1)} %copy-done.27), calls=%async_computation.2 | async-start | bytes 1572864 | tf_op jit(solution)/shard_map/all_to_all | solution.py:880
  70.1 14.1 %copy-start.18 = (bf16[768,768]{1,0:T(8,128)(2,1)S(1)}, bf16[768,768]{1,0:T(8,128)(2,1)}, u32[]{:S(2)}) copy-start(bf16[768,768]{1,0:T(8,128)(2,1)} %refs_6_.1) | copy-start | bytes 3538948
  84.2 13.6 %copy-start.55 = (f32[1,3072]{1,0:T(1,128)}, f32[1,3072]{1,0:T(1,128)S(1)}, u32[]{:S(2)}) copy-start(f32[1,3072]{1,0:T(1,128)S(1)} %get-tuple-element.88) | copy-start | bytes 36868
  84.2 13.6 %copy-start.61 = (bf16[768,512]{1,0:T(8,128)(2,1)}, bf16[768,512]{1,0:T(8,128)(2,1)S(1)}, u32[]{:S(2)}) copy-start(bf16[768,512]{1,0:T(8,128)(2,1)S(1)} %get-tuple-element.90.lt) | copy-start | bytes 2359300
  102.9 16.1 %all-to-all-start.3 = ((bf16[8,96,512]{2,1,0:T(8,128)(2,1)}), bf16[8,96,512]{2,1,0:T(8,128)(2,1)S(1)}, u32[]{:S(2)}, u32[]{:S(2)}) async-start(bf16[8,96,512]{2,1,0:T(8,128)(2,1)} %bitcast.57), calls=%async_computation.3 | async-start | bytes 1572864 | tf_op jit(solution)/shard_map/all_to_all | solution.py:889
  106.4 118.7 %collective-permute-start.18 = (bf16[512,3072]{1,0:T(8,128)(2,1)}, bf16[512,3072]{1,0:T(8,128)(2,1)}, u32[]{:S(2)}, u32[]{:S(2)}) collective-permute-start(bf16[512,3072]{1,0:T(8,128)(2,1)} %get-tuple-element.58.act.refs_1_), channel_id=1, source_target_pairs={{0,1},{1,0},{2,3},{3,2},{4,5},{5,4},{6,7},{7,6},{8,9},{9,8},{10,11... | collective-permute-start | bytes 9437192 | tf_op jit(solution)/shard_map/ppermute | solution.py:818
  130.1 21.3 %all-to-all-start.4 = ((bf16[8,96,512]{2,1,0:T(8,128)(2,1)}), bf16[8,96,512]{2,1,0:T(8,128)(2,1)}, u32[]{:S(2)}, u32[]{:S(2)}) async-start(bf16[8,96,512]{2,1,0:T(8,128)(2,1)} %copy-done.25), calls=%async_computation.4 | async-start | bytes 1572864 | tf_op jit(solution)/shard_map/all_to_all | solution.py:909
  134.4 38.1 %collective-permute-start.3 = (bf16[512,768]{1,0:T(8,128)(2,1)S(1)}, bf16[512,768]{1,0:T(8,128)(2,1)S(1)}, u32[]{:S(2)}, u32[]{:S(2)}) collective-permute-start(bf16[512,768]{1,0:T(8,128)(2,1)S(1)} %get-tuple-element.77.refs_5_.refs_1_), channel_id=1, source_target_pairs={{0,1},{1,0},{2,3},{3,2},{4,5},{5,4},{6,7},{7,6},{8,9},{9,8},{10,11... | collective-permute-start | bytes 2359304 | tf_op jit(solution)/shard_map/ppermute | solution.py:818
  138.1 78.6 %collective-permute-start.14 = (bf16[512,1536]{1,0:T(8,128)(2,1)}, bf16[512,1536]{1,0:T(8,128)(2,1)}, u32[]{:S(2)}, u32[]{:S(2)}) collective-permute-start(bf16[512,1536]{1,0:T(8,128)(2,1)} %get-tuple-element.62.refs_1_), channel_id=1, source_target_pairs={{0,1},{1,0},{2,3},{3,2},{4,5},{5,4},{6,7},{7,6},{8,9},{9,8},{10,11... | collective-permute-start | bytes 4718600 | tf_op jit(solution)/shard_map/ppermute | solution.py:818
  138.3 48.8 %collective-permute-start = (bf16[384,512]{1,0:T(8,128)(2,1)}, bf16[384,512]{1,0:T(8,128)(2,1)}, u32[]{:S(2)}, u32[]{:S(2)}) collective-permute-start(bf16[384,512]{1,0:T(8,128)(2,1)} %copy-done.63), channel_id=1, source_target_pairs={{0,1},{1,0},{2,3},{3,2},{4,5},{5,4},{6,7},{7,6},{8,9},{9,8},{10,11... | collective-permute-start | bytes 1179656 | tf_op jit(solution)/shard_map/ppermute | solution.py:818
  138.7 51.7 %collective-permute-start.1 = (bf16[512,768]{1,0:T(8,128)(2,1)}, bf16[512,768]{1,0:T(8,128)(2,1)}, u32[]{:S(2)}, u32[]{:S(2)}) collective-permute-start(bf16[512,768]{1,0:T(8,128)(2,1)} %copy-done.19), channel_id=1, source_target_pairs={{0,1},{1,0},{2,3},{3,2},{4,5},{5,4},{6,7},{7,6},{8,9},{9,8},{10,11... | collective-permute-start | bytes 2359304 | tf_op jit(solution)/shard_map/ppermute | solution.py:818
  151.4 31.5 %all-to-all-start.8 = ((f32[32,1,768]{2,1,0:T(1,128)}), f32[32,1,768]{2,1,0:T(1,128)}, u32[]{:S(2)}, u32[]{:S(2)}) async-start(f32[32,1,768]{2,1,0:T(1,128)} %reshape.160), calls=%async_computation.8 | async-start | bytes 196608 | tf_op jit(solution)/shard_map/all_to_all | solution.py:840
  163.6 8.9 %copy-start.3 = (bf16[768,2304]{1,0:T(8,128)(2,1)S(1)}, bf16[768,2304]{1,0:T(8,128)(2,1)}, u32[]{:S(2)}) copy-start(bf16[768,2304]{1,0:T(8,128)(2,1)} %weight.1) | copy-start | bytes 10616836
  163.6 8.9 %copy-start.17 = (f32[512,768]{1,0:T(8,128)S(1)}, f32[512,768]{1,0:T(8,128)}, u32[]{:S(2)}) copy-start(f32[512,768]{1,0:T(8,128)} %copy-done.16) | copy-start | bytes 4718596
  163.6 8.9 %copy-start.29 = (bf16[512,768]{1,0:T(8,128)(2,1)S(1)}, bf16[512,768]{1,0:T(8,128)(2,1)}, u32[]{:S(2)}) copy-start(bf16[512,768]{1,0:T(8,128)(2,1)} %copy-done.28) | copy-start | bytes 2359300
  163.6 8.9 %copy-start.31 = (bf16[512,768]{1,0:T(8,128)(2,1)S(1)}, bf16[512,768]{1,0:T(8,128)(2,1)}, u32[]{:S(2)}) copy-start(bf16[512,768]{1,0:T(8,128)(2,1)} %copy-done.30) | copy-start | bytes 2359300
  172.5 17.7 %collective-permute-start.2 = (bf16[384,512]{1,0:T(8,128)(2,1)}, bf16[384,512]{1,0:T(8,128)(2,1)}, u32[]{:S(2)}, u32[]{:S(2)}) collective-permute-start(bf16[384,512]{1,0:T(8,128)(2,1)} %get-tuple-element.78), channel_id=1, source_target_pairs={{0,1},{1,0},{2,3},{3,2},{4,5},{5,4},{6,7},{7,6},{8,9},{9,8},{10,11... | collective-permute-start | bytes 1179656 | tf_op jit(solution)/shard_map/ppermute | solution.py:818
  182.9 14.9 %all-to-all-start.7 = ((bf16[8,96,256]{2,1,0:T(8,128)(2,1)}), bf16[8,96,256]{2,1,0:T(8,128)(2,1)}, u32[]{:S(2)}, u32[]{:S(2)}) async-start(bf16[8,96,256]{2,1,0:T(8,128)(2,1)} %copy-done.40), calls=%async_computation.7 | async-start | bytes 786432 | tf_op jit(solution)/shard_map/all_to_all | solution.py:912
  187.1 51.8 %all-reduce.2.cloned.1.call-start = ((), (), s32[]{:S(2)}) async-start(), calls=%async_computation.11 | async-start | bytes 786432 | tf_op jit(solution)/shard_map/psum | solution.py:914
  187.2 10.6 %collective-permute-start.6 = (bf16[384,512]{1,0:T(8,128)(2,1)}, bf16[384,512]{1,0:T(8,128)(2,1)}, u32[]{:S(2)}, u32[]{:S(2)}) collective-permute-start(bf16[384,512]{1,0:T(8,128)(2,1)} %copy-done.64), channel_id=1, source_target_pairs={{0,1},{1,0},{2,3},{3,2},{4,5},{5,4},{6,7},{7,6},{8,9},{9,8},{10,11... | collective-permute-start | bytes 1179656 | tf_op jit(solution)/shard_map/ppermute | solution.py:818
  190.2 26.1 %collective-permute-start.13 = (bf16[768,512]{1,0:T(8,128)(2,1)}, bf16[768,512]{1,0:T(8,128)(2,1)}, u32[]{:S(2)}, u32[]{:S(2)}) collective-permute-start(bf16[768,512]{1,0:T(8,128)(2,1)} %copy-done.61), channel_id=1, source_target_pairs={{0,1},{1,0},{2,3},{3,2},{4,5},{5,4},{6,7},{7,6},{8,9},{9,8},{10,11... | collective-permute-start | bytes 2359304 | tf_op jit(solution)/shard_map/ppermute | solution.py:818
  195.9 16.6 %collective-permute-start.4 = (bf16[2,192,768]{2,1,0:T(8,128)(2,1)}, bf16[2,192,768]{2,1,0:T(8,128)(2,1)}, u32[]{:S(2)}, u32[]{:S(2)}) collective-permute-start(bf16[2,192,768]{2,1,0:T(8,128)(2,1)} %get-tuple-element.80), channel_id=1, source_target_pairs={{0,2},{1,3},{2,0},{3,1},{4,6},{5,7},{6,4},{7,5},{8,10},{9,11},{10,... | collective-permute-start | bytes 1769480 | tf_op jit(solution)/shard_map/ppermute | solution.py:818
  197.8 8.4 %collective-permute-start.7 = (bf16[384,512]{1,0:T(8,128)(2,1)}, bf16[384,512]{1,0:T(8,128)(2,1)S(1)}, u32[]{:S(2)}, u32[]{:S(2)}) collective-permute-start(bf16[384,512]{1,0:T(8,128)(2,1)} %get-tuple-element.84), channel_id=1, source_target_pairs={{0,1},{1,0},{2,3},{3,2},{4,5},{5,4},{6,7},{7,6},{8,9},{9,8},{10,11... | collective-permute-start | bytes 1179656 | tf_op jit(solution)/shard_map/ppermute | solution.py:818
  201.1 39.7 %all-to-all-start.5 = ((f32[32,1,576]{2,1,0:T(1,128)}), f32[32,1,576]{2,1,0:T(1,128)S(1)}, u32[]{:S(2)}, u32[]{:S(2)}) async-start(f32[32,1,576]{2,1,0:T(1,128)} %reshape.157), calls=%async_computation.5 | async-start | bytes 163840 | tf_op jit(solution)/shard_map/all_to_all | solution.py:840
  206.2 18.9 %collective-permute-start.17 = (bf16[384,512]{1,0:T(8,128)(2,1)}, bf16[384,512]{1,0:T(8,128)(2,1)S(1)}, u32[]{:S(2)}, u32[]{:S(2)}) collective-permute-start(bf16[384,512]{1,0:T(8,128)(2,1)} %bitcast.63), channel_id=1, source_target_pairs={{0,1},{1,0},{2,3},{3,2},{4,5},{5,4},{6,7},{7,6},{8,9},{9,8},{10,11... | collective-permute-start | bytes 1179656 | tf_op jit(solution)/shard_map/ppermute | solution.py:818
  212.5 20.2 %collective-permute-start.8 = (bf16[2,192,768]{2,1,0:T(8,128)(2,1)S(1)}, bf16[2,192,768]{2,1,0:T(8,128)(2,1)S(1)}, u32[]{:S(2)}, u32[]{:S(2)}) collective-permute-start(bf16[2,192,768]{2,1,0:T(8,128)(2,1)S(1)} %get-tuple-element.86), channel_id=1, source_target_pairs={{0,4},{1,5},{2,6},{3,7},{4,0},{5,1},{6,2},{7,3},{8,12},{9,13},{10,... | collective-permute-start | bytes 1769480 | tf_op jit(solution)/shard_map/ppermute | solution.py:818
  216.3 8.8 %copy-start.41 = (bf16[4,1,96,512]{3,2,1,0:T(8,128)(2,1)S(1)}, bf16[4,1,96,512]{3,2,1,0:T(8,128)(2,1)}, u32[]{:S(2)}) copy-start(bf16[4,1,96,512]{3,2,1,0:T(8,128)(2,1)} %get-tuple-element.147) | copy-start | bytes 1179652
  216.3 24.6 %collective-permute-start.5 = (bf16[1,192,768]{2,1,0:T(8,128)(2,1)}, bf16[1,192,768]{2,1,0:T(8,128)(2,1)}, u32[]{:S(2)}, u32[]{:S(2)}) collective-permute-start(bf16[1,192,768]{2,1,0:T(8,128)(2,1)} %slice.139), channel_id=1, source_target_pairs={{0,4},{1,5},{2,6},{3,7},{4,0},{5,1},{6,2},{7,3},{8,12},{9,13},{10,... | collective-permute-start | bytes 884744 | tf_op jit(solution)/shard_map/ppermute | solution.py:818
  223.8 47.4 %collective-permute-start.15 = (bf16[2,768,384]{2,1,0:T(8,128)(2,1)}, bf16[2,768,384]{2,1,0:T(8,128)(2,1)}, u32[]{:S(2)}, u32[]{:S(2)}) collective-permute-start(bf16[2,768,384]{2,1,0:T(8,128)(2,1)} %get-tuple-element.92), channel_id=1, source_target_pairs={{0,4},{1,5},{2,6},{3,7},{4,0},{5,1},{6,2},{7,3},{8,12},{9,13},{10,... | collective-permute-start | bytes 3538952 | tf_op jit(solution)/shard_map/ppermute | solution.py:818
  231.2 43.3 %collective-permute-start.19 = (bf16[2,96,3072]{2,1,0:T(8,128)(2,1)}, bf16[2,96,3072]{2,1,0:T(8,128)(2,1)}, u32[]{:S(2)}, u32[]{:S(2)}) collective-permute-start(bf16[2,96,3072]{2,1,0:T(8,128)(2,1)} %get-tuple-element.94), channel_id=1, source_target_pairs={{0,2},{1,3},{2,0},{3,1},{4,6},{5,7},{6,4},{7,5},{8,10},{9,11},{10,... | collective-permute-start | bytes 3538952 | tf_op jit(solution)/shard_map/ppermute | solution.py:818
  234.4 29.4 %collective-permute-start.9 = (bf16[1,192,768]{2,1,0:T(8,128)(2,1)}, bf16[1,192,768]{2,1,0:T(8,128)(2,1)}, u32[]{:S(2)}, u32[]{:S(2)}) collective-permute-start(bf16[1,192,768]{2,1,0:T(8,128)(2,1)} %slice.141), channel_id=1, source_target_pairs={{0,2},{1,3},{2,0},{3,1},{4,6},{5,7},{6,4},{7,5},{8,10},{9,11},{10,... | collective-permute-start | bytes 884744 | tf_op jit(solution)/shard_map/ppermute | solution.py:818
  266.2 20.2 %all-to-all-start.6 = ((bf16[4,384,192]{1,2,0:T(8,128)(2,1)}), bf16[4,384,192]{1,2,0:T(8,128)(2,1)S(1)}, u32[]{:S(2)}, u32[]{:S(2)}) async-start(bf16[4,384,192]{1,2,0:T(8,128)(2,1)} %maximum_bitcast_fusion), calls=%async_computation.6 | async-start | bytes 1179648 | tf_op jit(solution)/shard_map/all_to_all | solution.py:833
  272.9 12.5 %collective-permute-start.16 = (bf16[1,768,384]{2,1,0:T(8,128)(2,1)S(1)}, bf16[1,768,384]{2,1,0:T(8,128)(2,1)S(1)}, u32[]{:S(2)}, u32[]{:S(2)}) collective-permute-start(bf16[1,768,384]{2,1,0:T(8,128)(2,1)S(1)} %slice.147), channel_id=1, source_target_pairs={{0,2},{1,3},{2,0},{3,1},{4,6},{5,7},{6,4},{7,5},{8,10},{9,11},{10,... | collective-permute-start | bytes 1769480 | tf_op jit(solution)/shard_map/ppermute | solution.py:818
  277.0 15.7 %collective-permute-start.20 = (bf16[1,96,3072]{2,1,0:T(8,128)(2,1)}, bf16[1,96,3072]{2,1,0:T(8,128)(2,1)}, u32[]{:S(2)}, u32[]{:S(2)}) collective-permute-start(bf16[1,96,3072]{2,1,0:T(8,128)(2,1)} %slice.149), channel_id=1, source_target_pairs={{0,4},{1,5},{2,6},{3,7},{4,0},{5,1},{6,2},{7,3},{8,12},{9,13},{10,... | collective-permute-start | bytes 1769480 | tf_op jit(solution)/shard_map/ppermute | solution.py:818
  286.3 16.9 %all-to-all-start.9 = ((bf16[4,192,384]{2,1,0:T(8,128)(2,1)}), bf16[4,192,384]{2,1,0:T(8,128)(2,1)S(1)}, u32[]{:S(2)}, u32[]{:S(2)}) async-start(bf16[4,192,384]{2,1,0:T(8,128)(2,1)} %bitcast.24), calls=%async_computation.9 | async-start | bytes 1179648 | tf_op jit(solution)/shard_map/all_to_all | solution.py:833
  303.3 16.5 %all-to-all-start.10 = ((bf16[4,96,768]{2,1,0:T(8,128)(2,1)}), bf16[4,96,768]{2,1,0:T(8,128)(2,1)S(1)}, u32[]{:S(2)}, u32[]{:S(2)}) async-start(bf16[4,96,768]{2,1,0:T(8,128)(2,1)} %bitcast.49), calls=%async_computation.10 | async-start | bytes 1179648 | tf_op jit(solution)/shard_map/all_to_all | solution.py:833
  306.9 6.0 %collective-permute-start.12 = (bf16[96,192]{1,0:T(8,128)(2,1)S(1)}, bf16[96,192]{1,0:T(8,128)(2,1)S(1)}, u32[]{:S(2)}, u32[]{:S(2)}) collective-permute-start(bf16[96,192]{1,0:T(8,128)(2,1)S(1)} %get-tuple-element.152), channel_id=1, source_target_pairs={{2,0},{5,1},{0,2},{3,3},{6,4},{1,5},{4,6},{7,7},{10,8},{13,9},{8,1... | collective-permute-start | bytes 110600 | tf_op jit(solution)/shard_map/ppermute | solution.py:931
  310.2 2.6 collective-permute-start.11
  310.3 2.5 collective-permute-start.10
  (69 other events, 170.8 us)
Sparse Core Ops, SparseCore 0:
  200.1 38.7 all-reduce.1
